TPU v7x, 128 devices: a whole 4x4x4 slice. The times are simulated.
128 devices in a mesh: gx: 8 (over z, core), gy: 16 (over x, y).
Axes of the slice: x: 4, y: 4, z: 4, core: 2. Of those that a mesh axis runs over, the one named last changes fastest.
Arguments:
- tokens: bfloat16 [64, 14848], P(None, ('gy', 'gx'))
- lengths: int32 [64], P('gy'), may hold values from 1 to 4096, as said below
- gain_attn: float32 [14848], P('gy'), may hold values from 0.1 to 1.9
- bias_attn: float32 [14848], P('gy'), may hold values from -1.5 to 1.5
- gain_mlp: float32 [14848], P('gy'), may hold values from 0.1 to 1.9
- bias_mlp: float32 [14848], P('gy'), may hold values from -1.5 to 1.5
- w_qkv: bfloat16 [14848, 15872], P('gy', 'gx'), may hold values from -0.046875 to 0.046875
- w_out: bfloat16 [14848, 14848], P('gx', 'gy'), may hold values from -0.046875 to 0.046875
- w_up: bfloat16 [14848, 29696], P('gy', 'gx'), may hold values from -0.046875 to 0.046875
- w_down: bfloat16 [29696, 14848], P('gx', 'gy'), may hold values from -0.03125 to 0.03125
- cache: bfloat16 [64, 8, 4096, 128], P('gy', 'gx')
Outputs:
- mixed: bfloat16 [64, 14848], P(None, ('gy', 'gx'))
- new_kv: bfloat16 [64, 8, 128], P('gy', 'gx')
Inputs may be any that keep to these rules, and one draw needn't show every extreme that they name: Row r's cache holds lengths[r] valid slots at its start; the slots after them hold values that must be ignored. Some row in every draw has all 4096 slots valid.
All inputs are finite; a program needn't handle non-finite values.
Results may differ from a plain program's by a relative error of at most 0.035.
Values may be sent and summed in bfloat16 or wider, within the bound.
No kernel may reach another device: no remote copies, remote signals or barrier semaphores. Data moves between devices by JAX's collectives and lax.ppermute only.
A program may use at most 128 MiB of HBM per device.

v0:
```python
import math

import jax
import jax.numpy as jnp
from jax import lax
from jax.sharding import PartitionSpec as P

HD = 64
QPG = 29


EPS = 1e-05
THETA = 10000.0


def rotate(u, angle):
    half = u.shape[-1] // 2
    first = u[..., :half]
    second = u[..., half:]
    cosine = jnp.cos(angle)
    sine = jnp.sin(angle)
    return jnp.concatenate(
        [first * cosine - second * sine, second * cosine + first * sine], axis=-1
    )


def angles(lengths, head_dim):
    steps = jnp.arange(head_dim // 2, dtype=jnp.float32) * (2.0 / head_dim)
    inverse = jnp.power(jnp.float32(THETA), -steps)
    return lengths.astype(jnp.float32)[:, None] * inverse[None, :]


def normalize(values, mean, scale, gain, bias):
    centred = (values - mean[:, None]) * scale[:, None]
    return (centred * gain + bias).astype(jnp.bfloat16)


def attend_local(query, key_new, value_new, cache, lengths):
    head_dim = query.shape[-1]
    scale = 1.0 / math.sqrt(head_dim)
    keys = cache[..., :head_dim]
    values = cache[..., head_dim:]
    scores = jnp.einsum("rgqd,rgtd->rgqt", query, keys, preferred_element_type=jnp.float32) * scale
    positions = jnp.arange(cache.shape[2], dtype=jnp.int32)
    live = positions[None, None, None, :] < lengths[:, None, None, None]
    scores = jnp.where(live, scores, -1e30)
    own = jnp.einsum("rgqd,rgd->rgq", query, key_new, preferred_element_type=jnp.float32) * scale
    top = jnp.maximum(jnp.max(scores, axis=-1), own)
    probs = jnp.where(live, jnp.exp(scores - top[..., None]), 0.0)
    own_prob = jnp.exp(own - top)
    total = jnp.sum(probs, axis=-1) + own_prob
    weights = probs.astype(jnp.bfloat16)
    own_weight = own_prob.astype(jnp.bfloat16).astype(jnp.float32)
    summed = jnp.einsum("rgqt,rgtd->rgqd", weights, values, preferred_element_type=jnp.float32)
    summed = summed + own_weight[..., None] * value_new.astype(jnp.float32)[:, :, None, :]
    result = (summed / total[..., None]).astype(jnp.bfloat16)
    return result.reshape(result.shape[0], -1)


def local(
    tokens, lengths, gain_attn, bias_attn, gain_mlp, bias_mlp, w_qkv, w_out, w_up, w_down, cache
):
    size_gx = lax.axis_size("gx")
    size_gy = lax.axis_size("gy")
    rows = tokens.shape[0]
    narrow = tokens.shape[1]
    width = narrow * size_gx * size_gy
    values = tokens.astype(jnp.float32)
    totals, squares = lax.psum(
        (jnp.sum(values, axis=1), jnp.sum(values * values, axis=1)), ("gx", "gy")
    )
    mean = totals / width
    scale = 1.0 / jnp.sqrt(squares / width - mean * mean + EPS)
    offset = lax.axis_index("gx") * narrow
    part_gain_a = lax.dynamic_slice_in_dim(gain_attn, offset, narrow)
    part_bias_a = lax.dynamic_slice_in_dim(bias_attn, offset, narrow)
    part_gain_m = lax.dynamic_slice_in_dim(gain_mlp, offset, narrow)
    part_bias_m = lax.dynamic_slice_in_dim(bias_mlp, offset, narrow)
    h_attn, h_mlp = (
        lax.all_gather(
            normalize(values, mean, scale, part_gain_a, part_bias_a), "gx", axis=1, tiled=True
        ),
        lax.all_gather(
            normalize(values, mean, scale, part_gain_m, part_bias_m), "gx", axis=1, tiled=True
        ),
    )
    local_rows = rows // size_gy
    qkv = lax.psum_scatter(
        jnp.dot(h_attn, w_qkv, preferred_element_type=jnp.float32).astype(jnp.bfloat16),
        "gy",
        scatter_dimension=0,
        tiled=True,
    )
    groups = cache.shape[1]
    qkv = qkv.reshape(local_rows, groups, QPG + 2, HD)
    angle = angles(lengths, HD)
    query = rotate(qkv[:, :, :QPG].astype(jnp.float32), angle[:, None, None, :]).astype(
        jnp.bfloat16
    )
    key_new = rotate(qkv[:, :, QPG].astype(jnp.float32), angle[:, None, :]).astype(jnp.bfloat16)
    value_new = qkv[:, :, QPG + 1]
    new_kv = jnp.concatenate([key_new, value_new], axis=-1)
    attn = attend_local(query, key_new, value_new, cache, lengths)
    attn_part = jnp.dot(
        lax.all_gather(attn, "gy", axis=0, tiled=True), w_out, preferred_element_type=jnp.float32
    )
    up = jnp.dot(h_mlp, w_up, preferred_element_type=jnp.float32)
    share = lax.psum_scatter(up.astype(jnp.bfloat16), "gy", scatter_dimension=1, tiled=True).astype(
        jnp.float32
    )
    hidden = jax.nn.gelu(share, approximate=False).astype(jnp.bfloat16)
    mlp_part = jnp.dot(
        lax.all_gather(hidden, "gy", axis=1, tiled=True), w_down, preferred_element_type=jnp.float32
    )
    merged = lax.psum_scatter(
        (attn_part + mlp_part).astype(jnp.bfloat16), "gx", scatter_dimension=1, tiled=True
    ).astype(jnp.float32)
    mixed = (values + merged).astype(jnp.bfloat16)
    return (mixed, new_kv)


def solution(mesh):
    in_specs = (
        P(None, ("gy", "gx")),
        P("gy"),
        P("gy"),
        P("gy"),
        P("gy"),
        P("gy"),
        P("gy", "gx"),
        P("gx", "gy"),
        P("gy", "gx"),
        P("gx", "gy"),
        P("gy", "gx", None, None),
    )
    out_specs = (P(None, ("gy", "gx")), P("gy", "gx", None))
    return jax.shard_map(local, mesh=mesh, in_specs=in_specs, out_specs=out_specs, check_vma=False)
```

profile of v0, /device:TPU:1, one launch (start us, length us, event | category | flops | bytes accessed | tf_op | source)
XLA Modules:
  0.0 326.9 jit_solution(3947512679297426584)
XLA Ops:
  7.2 0.0 all-reduce.10.cloned.1.call-start
  7.2 0.8 dynamic_slice.12
  8.0 0.8 dynamic_slice.13
  8.7 0.8 dynamic_slice.14
  9.5 0.8 dynamic_slice.15
  10.3 0.8 convert_reduce_fusion
  11.1 68.7 %all-reduce.3 = (f32[64]{0:T(128)S(1)}, f32[64]{0:T(128)S(1)}) all-reduce(f32[64]{0:T(128)S(1)} %get-tuple-element.3, f32[64]{0:T(128)S(1)} %get-tuple-element.2), channel_id=1, replica_groups=mesh['gx'=8,'gy'=16] {'gx','gy'}, use_global_device_ids=true, to_apply=%region_3.0 | all-reduce | flops 128 | bytes 1024 | tf_op jit(solution)/shard_map/psum | solution.py:69
  79.8 0.8 fusion.65
  80.6 13.5 %all-gather.2 = bf16[8,116,64]{1,2,0:T(8,128)(2,1)S(1)} all-gather(bf16[1,116,64]{1,2,0:T(8,128)(2,1)S(1)} %get-tuple-element.13), channel_id=1, replica_groups=mesh['gx'=8,'gy'=16] {'gx'}, dimensions={0}, use_global_device_ids=true | all-gather | bytes 133632 | tf_op jit(solution)/shard_map/all_gather | solution.py:83
  94.1 0.1 copy.24
  94.2 0.2 reshape.305
  94.3 12.8 %all-gather = bf16[8,116,64]{1,2,0:T(8,128)(2,1)S(1)} all-gather(bf16[1,116,64]{1,2,0:T(8,128)(2,1)S(1)} %get-tuple-element.14), channel_id=1, replica_groups=mesh['gx'=8,'gy'=16] {'gx'}, dimensions={0}, use_global_device_ids=true | all-gather | bytes 133632 | tf_op jit(solution)/shard_map/all_gather | solution.py:80
  107.1 0.1 copy.21
  107.2 0.2 reshape.301
  107.3 3.6 %convolution_convert_fusion.1 = bf16[64,1984]{1,0:T(8,128)(2,1)} fusion(bf16[928,64]{0,1:T(8,128)(2,1)S(1)} %reshape.301, bf16[928,1984]{1,0:T(8,128)(2,1)} %param.17), kind=kOutput, calls=%fused_computation.8 | convolution fusion | flops 235794432 | bytes 4055040 | tf_op jit(solution)/shard_map/dot_general | solution.py:89
  110.9 0.0 copy-start.4
  110.9 0.0 copy-start.3
  110.9 0.0 copy-start.2
  110.9 5.1 %convolution_convert_fusion = bf16[64,3712]{1,0:T(8,128)(2,1)} fusion(bf16[928,64]{0,1:T(8,128)(2,1)S(1)} %reshape.305, bf16[928,3712]{1,0:T(8,128)(2,1)} %param.19), kind=kOutput, calls=%fused_computation.2 | convolution fusion | flops 441163776 | bytes 7483392 | tf_op jit(solution)/shard_map/dot_general | solution.py:107
  116.0 0.0 all-reduce.10.cloned.1.call-update
  116.1 0.0 all-reduce.8.cloned.1.call-start
  116.1 0.0 copy-done.4
  116.2 0.6 dynamic-slice.4
  116.7 0.0 copy-done.3
  116.7 0.6 dynamic-slice
  118.6 0.0 copy-done.2
  119.3 0.1 multiply_cosine_fusion.1
  119.4 0.1 iota_compare_fusion
  119.5 77.7 %all-reduce.10.cloned.1.call-done = (bf16[64,1984]{1,0:T(8,128)(2,1)}, bf16[64,3712]{1,0:T(8,128)(2,1)}) async-done(((bf16[64,1984]{1,0:T(8,128)(2,1)}, bf16[64,3712]{1,0:T(8,128)(2,1)}), (bf16[64,1984]{1,0:T(8,128)(2,1)}, bf16[64,3712]{1,0:T(8,128)(2,1)})) %all-reduce.10.cloned.1.call-update) | async-done | bytes 729104
  197.2 0.8 constant_dynamic-slice_fusion
  198.0 0.1 reshape.294
  198.1 0.1 fusion.73
  198.2 1.0 fusion.64
  199.3 16.7 %all-gather.3 = bf16[16,232,64]{1,2,0:T(8,128)(2,1)S(1)} all-gather(bf16[1,232,64]{1,2,0:T(8,128)(2,1)S(1)} %fusion.64), channel_id=1, replica_groups=mesh['gx'=8,'gy'=16] {'gy'}, dimensions={0}, use_global_device_ids=true | all-gather | bytes 504832 | tf_op jit(solution)/shard_map/all_gather | solution.py:113
  215.9 0.3 copy.25
  216.2 0.7 reshape.307
  217.0 0.1 maximum_bitcast_fusion
  217.0 0.1 fusion.62
  217.1 0.2 fusion.67
  217.3 0.0 copy-start
  217.3 4.0 %fusion.82 = (f32[4,29]{1,0:T(4,128)S(1)}, f32[4,29,4096]{2,1,0:T(8,128)S(1)}) fusion(bf16[4,1,4096,128]{3,2,1,0:T(8,128)(2,1)} %param.21, bf16[4,29,32]{2,1,0:T(8,128)(2,1)S(1)} %get-tuple-element.9, bf16[4,29,32]{2,1,0:T(8,128)(2,1)S(1)} %get-tuple-element.8, pred[4,4096]{1,0:T(4,128)(4,1)S(1)} %iota_compare_fusion), kind=kOutput, calls=%fused_computation.108 | convolution fusion | flops 62272396 | bytes 6126544 | tf_op jit(solution)/shard_map/rgqd,rgtd->rgqt/dot_general | solution.py:43
  221.3 0.6 fusion.6
  222.0 0.0 copy-done
  222.0 1.6 fusion.15
  223.6 0.1 reshape.302
  223.7 17.2 %all-gather.1 = bf16[16,4,1856]{2,1,0:T(4,128)(2,1)S(1)} all-gather(bf16[1,4,1856]{2,1,0:T(4,128)(2,1)S(1)} %reshape.302), channel_id=1, replica_groups=mesh['gx'=8,'gy'=16] {'gy'}, dimensions={0}, use_global_device_ids=true | all-gather | bytes 252416 | tf_op jit(solution)/shard_map/all_gather | solution.py:105
  240.9 0.1 reshape.303
  241.0 3.2 fusion.83
  244.2 0.0 copy-start.1
  244.2 5.7 %fusion.8 = bf16[64,928]{1,0:T(8,128)(2,1)} fusion(f32[64,928]{1,0:T(8,128)S(1)} %fusion.83, bf16[3712,64]{0,1:T(8,128)(2,1)S(1)} %reshape.307, bf16[3712,928]{0,1:T(8,128)(2,1)} %param.20), kind=kOutput, calls=%fused_computation.13 | convolution fusion | flops 441044992 | bytes 7720960 | tf_op jit(solution)/shard_map/dot_general | solution.py:112
  249.9 0.0 all-reduce.8.cloned.1.call-update
  249.9 0.6 pad_maximum_fusion.3
  250.5 68.1 %all-reduce.8.cloned.1.call-done = bf16[64,928]{1,0:T(8,128)(2,1)} async-done(((bf16[64,928]{1,0:T(8,128)(2,1)}), bf16[64,928]{1,0:T(8,128)(2,1)}) %all-reduce.8.cloned.1.call-update) | async-done | bytes 118800
  318.7 0.0 copy-done.1
  318.7 1.4 fusion.61
  (8 shorter events, 0.1 us)
Async XLA Ops:
  7.2 190.0 %all-reduce.10.cloned.1.call-start = ((), (), s32[]{:S(2)}) async-start(), calls=%async_computation.1 | async-start | bytes 1474560
  110.9 5.2 %copy-start.4 = (u32[128]{0:T(128)S(1)}, u32[128]{0:T(128)}, u32[]{:S(2)}) copy-start(u32[128]{0:T(128)} %constant.104) | copy-start | bytes 1540
  110.9 5.8 %copy-start.3 = (u32[128]{0:T(128)S(1)}, u32[128]{0:T(128)}, u32[]{:S(2)}) copy-start(u32[128]{0:T(128)} %constant.96) | copy-start | bytes 1540
  110.9 7.7 %copy-start.2 = (s32[4]{0:T(128)S(1)}, s32[4]{0:T(128)}, u32[]{:S(2)}) copy-start(s32[4]{0:T(128)} %param.12) | copy-start | bytes 52
  116.1 202.6 %all-reduce.8.cloned.1.call-start = ((), (), s32[]{:S(2)}) async-start(), calls=%async_computation | async-start | bytes 262144
  217.3 4.6 %copy-start = (bf16[4,1,4096,128]{3,2,1,0:T(8,128)(2,1)S(1)}, bf16[4,1,4096,128]{3,2,1,0:T(8,128)(2,1)}, u32[]{:S(2)}) copy-start(bf16[4,1,4096,128]{3,2,1,0:T(8,128)(2,1)} %param.21) | copy-start | bytes 12582916
  244.2 74.5 %copy-start.1 = (bf16[64,116]{1,0:T(8,128)(2,1)S(1)}, bf16[64,116]{1,0:T(8,128)(2,1)}, u32[]{:S(2)}) copy-start(bf16[64,116]{1,0:T(8,128)(2,1)} %param.11) | copy-start | bytes 44548
Sparse Core Ops, SparseCore 0:
  116.2 80.9 all-reduce.9
  250.0 68.5 all-reduce.7
where the time goes:
time: 329 us; the launch traced here: 327 us
  waiting for transfers between devices  146 us (44%)
  blocking collectives  129 us (39%)
  matrix products  23.4 us (7%)
  between operations  16.2 us (5%)
  local copies, waits for them, and re-layouts  6.8 us (2%)
  other arithmetic  5.89 us (2%)
    unnamed x4, waiting for transfers between devices  146 us
    psum x1, blocking collectives, local(): lax.psum((jnp.sum(values, axis=1), jnp.sum(values * values, axis=1)), ('g...  68.7 us
    all_gather x1, blocking collectives, local(): lax.all_gather(attn, 'gy', axis=0, tiled=True)  17.2 us
    all_gather x1, blocking collectives, local(): lax.all_gather(hidden, 'gy', axis=1, tiled=True)  16.7 us
    all_gather x1, blocking collectives, local(): lax.all_gather(normalize(values, mean, scale, part_gain_m, part_bias_m),...  13.5 us
    all_gather x1, blocking collectives, local(): lax.all_gather(normalize(values, mean, scale, part_gain_a, part_bias_a),...  12.8 us
  transfers between devices with their start and end apart: 2, of which 2 were waited for; matrix products, arithmetic and copies ran while one was open for 1% of the time, Pallas kernels for 0%

commit v1 on v0

v1 whole, which is shorter than its diff:
```python
import math

import jax
import jax.numpy as jnp
from jax import lax
from jax.sharding import PartitionSpec as P

HD = 64
QPG = 29
EPS = 1e-05
THETA = 10000.0
BF = jnp.bfloat16
F32 = jnp.float32


def rotate(u, angle):
    half = u.shape[-1] // 2
    first = u[..., :half]
    second = u[..., half:]
    cosine = jnp.cos(angle)
    sine = jnp.sin(angle)
    return jnp.concatenate(
        [first * cosine - second * sine, second * cosine + first * sine], axis=-1
    )


def angles(lengths, head_dim):
    steps = jnp.arange(head_dim // 2, dtype=F32) * (2.0 / head_dim)
    inverse = jnp.power(F32(THETA), -steps)
    return lengths.astype(F32)[:, None] * inverse[None, :]


def attend_local(query, key_new, value_new, cache, lengths):
    head_dim = query.shape[-1]
    scale = 1.0 / math.sqrt(head_dim)
    keys = cache[..., :head_dim]
    values = cache[..., head_dim:]
    scores = jnp.einsum("rgqd,rgtd->rgqt", query, keys, preferred_element_type=F32) * scale
    positions = jnp.arange(cache.shape[2], dtype=jnp.int32)
    live = positions[None, None, None, :] < lengths[:, None, None, None]
    scores = jnp.where(live, scores, -1e30)
    own = jnp.einsum("rgqd,rgd->rgq", query, key_new, preferred_element_type=F32) * scale
    top = jnp.maximum(jnp.max(scores, axis=-1), own)
    probs = jnp.where(live, jnp.exp(scores - top[..., None]), 0.0)
    own_prob = jnp.exp(own - top)
    total = jnp.sum(probs, axis=-1) + own_prob
    weights = probs.astype(BF)
    own_weight = own_prob.astype(BF).astype(F32)
    summed = jnp.einsum("rgqt,rgtd->rgqd", weights, values, preferred_element_type=F32)
    summed = summed + own_weight[..., None] * value_new.astype(F32)[:, :, None, :]
    result = (summed / total[..., None]).astype(BF)
    return result.reshape(result.shape[0], -1)


def pieces(value, count):
    out = []
    for _ in range(count):
        part = value.astype(BF)
        out.append(part)
        value = value - part.astype(F32)
    return out


def swap_core(x):
    return lax.ppermute(x, "gx", [(i, i ^ 1) for i in range(8)])


def shift_z(x, k):
    return lax.ppermute(x, "gx", [(i, (i + 2 * k) % 8) for i in range(8)])


def gather_tokens(tokens):
    core = lax.axis_index("gx") % 2
    z = lax.axis_index("gx") // 2
    other = swap_core(tokens)
    pair = jnp.stack([jnp.where(core == 0, tokens, other), jnp.where(core == 0, other, tokens)])
    got = [pair] + [shift_z(pair, k) for k in (1, 2, 3)]
    ring = jnp.stack([got[0], got[3], got[2], got[1]])
    ring = jnp.roll(ring, z, axis=0)
    return ring.reshape(8, *tokens.shape).transpose(1, 0, 2).reshape(tokens.shape[0], -1)


def local(
    tokens, lengths, gain_attn, bias_attn, gain_mlp, bias_mlp, w_qkv, w_out, w_up, w_down, cache
):
    rows = tokens.shape[0]
    size_gy = lax.axis_size("gy")
    own_rows = rows // size_gy
    wide = gain_attn.shape[0]
    width = wide * size_gy
    up_cols, qkv_cols = w_up.shape[1], w_qkv.shape[1]

    values = gather_tokens(tokens).astype(F32)
    part_sum = jnp.sum(values, axis=1)
    centre = part_sum / wide
    shifted = values - centre[:, None]
    part_square = jnp.sum(shifted * shifted, axis=1)

    def product(gain, bias, weight):
        left = jnp.concatenate(
            [
                (shifted * gain).astype(BF),
                jnp.stack(pieces(gain, 2) + pieces(bias, 2)),
            ]
        )
        out = jnp.dot(left, weight, preferred_element_type=F32)
        main = out[:rows].astype(BF).reshape(size_gy, own_rows, -1)
        vectors = jnp.stack(
            pieces(out[rows] + out[rows + 1], 2) + pieces(out[rows + 2] + out[rows + 3], 2)
        )
        vectors = jnp.broadcast_to(vectors[None], (size_gy,) + vectors.shape)
        return jnp.concatenate([main, vectors], axis=1)

    stats = jnp.stack(pieces(part_sum, 3) + pieces(part_square, 3), axis=-1)
    stats = stats.reshape(size_gy, own_rows, 6)
    stats = jnp.pad(stats, ((0, 0), (0, 4), (0, 58)))
    payload = jnp.concatenate(
        [product(gain_mlp, bias_mlp, w_up), product(gain_attn, bias_attn, w_qkv), stats], axis=2
    )
    got = lax.all_to_all(payload, "gy", 0, 0).astype(F32)

    stat = got[:, :own_rows, up_cols + qkv_cols :]
    sums = stat[..., 0] + stat[..., 1] + stat[..., 2]
    squares = stat[..., 3] + stat[..., 4] + stat[..., 5]
    mean = jnp.sum(sums, axis=0) / width
    gap = sums / wide - mean
    var = jnp.sum(squares + wide * gap * gap, axis=0) / width
    scale = 1.0 / jnp.sqrt(var + EPS)
    main = got[:, :own_rows, : up_cols + qkv_cols]
    gains = (got[:, 4] + got[:, 5])[:, None, : up_cols + qkv_cols]
    biases = (got[:, 6] + got[:, 7])[:, : up_cols + qkv_cols]
    full = scale[:, None] * jnp.sum(main + gap[..., None] * gains, axis=0) + jnp.sum(biases, axis=0)

    hidden = jax.nn.gelu(full[:, :up_cols], approximate=False).astype(BF)
    qkv = full[:, up_cols:].astype(BF).reshape(own_rows, 1, QPG + 2, HD)
    angle = angles(lengths, HD)
    query = rotate(qkv[:, :, :QPG].astype(F32), angle[:, None, None, :]).astype(BF)
    key_new = rotate(qkv[:, :, QPG].astype(F32), angle[:, None, :]).astype(BF)
    value_new = qkv[:, :, QPG + 1]
    new_kv = jnp.concatenate([key_new, value_new], axis=-1)
    attn = attend_local(query, key_new, value_new, cache, lengths)

    block = jnp.concatenate([hidden, attn], axis=1)
    block = jnp.broadcast_to(block[None], (size_gy,) + block.shape)
    every = lax.all_to_all(block, "gy", 0, 0).reshape(rows, -1)
    part = jnp.dot(every[:, :up_cols], w_down, preferred_element_type=F32) + jnp.dot(
        every[:, up_cols:], w_out, preferred_element_type=F32
    )

    core = lax.axis_index("gx") % 2
    z = lax.axis_index("gx") // 2
    blocks = part.reshape(rows, 4, 2, -1).transpose(2, 1, 0, 3)
    keep = jnp.where(core == 0, blocks[0], blocks[1])
    send = jnp.where(core == 0, blocks[1], blocks[0])
    keep = keep + swap_core(send)
    turned = jnp.roll(keep, -z, axis=0)
    narrow = turned.astype(BF)
    total = turned[0]
    for k in (1, 2, 3):
        total = total + shift_z(narrow[k], k).astype(F32)
    mixed = (tokens.astype(F32) + total).astype(BF)
    return (mixed, new_kv)


def solution(mesh):
    in_specs = (
        P(None, ("gy", "gx")),
        P("gy"),
        P("gy"),
        P("gy"),
        P("gy"),
        P("gy"),
        P("gy", "gx"),
        P("gx", "gy"),
        P("gy", "gx"),
        P("gx", "gy"),
        P("gy", "gx", None, None),
    )
    out_specs = (P(None, ("gy", "gx")), P("gy", "gx", None))
    return jax.shard_map(local, mesh=mesh, in_specs=in_specs, out_specs=out_specs, check_vma=False)
```

time: 329 us -> 194 us (0.59)
  waiting for transfers between devices: 146 us -> 26.3 us
  blocking collectives: 129 us -> 14.5 us
  other arithmetic: 5.89 us -> 95.4 us
  starting transfers between devices: 0.08 us -> 19.5 us
  between operations: 16.2 us -> 1.13 us
  local copies, waits for them, and re-layouts: 6.8 us -> 17 us
  matrix products: 23.4 us -> 19.3 us
    unnamed x4 -> x0, waiting for transfers between devices: 146 us -> none
    psum x1 -> x0, blocking collectives: 68.7 us -> none  [local(): lax.psum((jnp.sum(values, axis=1), jnp.sum(values * values, axis=1)), ('g...]
    all_gather x4 -> x0, blocking collectives: 60.1 us -> none  [the longest x1 17.2 us: local(): lax.all_gather(attn, 'gy', axis=0, tiled=True)]
    reduce_sum x1 -> x6, other arithmetic: 0.82 us -> 37.4 us  [the longest x1 34.5 us: local(): jnp.sum(main + gap[..., None] * gains, axis=0)]
    add x0 -> x3, other arithmetic: none -> 36.2 us  [the longest x1 36.1 us: local(): biases = (got[:, 6] + got[:, 7])[:, :up_cols + qkv_cols]]
    all_to_all x0 -> x1, waiting for transfers between devices: none -> 19.2 us  [local(): got = lax.all_to_all(payload, 'gy', 0, 0).astype(F32)]
    convert_element_type x4 -> x15, other arithmetic: 1.46 us -> 18.2 us  [the longest x1 13.3 us: local(): got = lax.all_to_all(payload, 'gy', 0, 0).astype(F32)]
    all_to_all x0 -> x1, blocking collectives: none -> 14.5 us  [local(): every = lax.all_to_all(block, 'gy', 0, 0).reshape(rows, -1)]
  transfers between devices with their start and end apart: 2 -> 9, of which waited for: 2 -> 6; matrix products, arithmetic and copies ran while one was open for 1% -> 2% of each run, Pallas kernels for 0% -> 0%
where the time goes in v1:
time: 194 us; the launch traced here: 193 us
  other arithmetic  95.4 us (49%)
  waiting for transfers between devices  26.3 us (14%)
  starting transfers between devices  19.5 us (10%)
  matrix products  19.3 us (10%)
  local copies, waits for them, and re-layouts  17 us (9%)
  blocking collectives  14.5 us (7%)
    add x1, other arithmetic, local(): biases = (got[:, 6] + got[:, 7])[:, :up_cols + qkv_cols]  36.1 us
    reduce_sum x1, other arithmetic, local(): jnp.sum(main + gap[..., None] * gains, axis=0)  34.5 us
    all_to_all x1, waiting for transfers between devices, local(): got = lax.all_to_all(payload, 'gy', 0, 0).astype(F32)  19.2 us
    all_to_all x1, blocking collectives, local(): every = lax.all_to_all(block, 'gy', 0, 0).reshape(rows, -1)  14.5 us
    convert_element_type x1, other arithmetic, local(): got = lax.all_to_all(payload, 'gy', 0, 0).astype(F32)  13.3 us
    all_to_all x1, local copies, waits for them, and re-layouts, local(): got = lax.all_to_all(payload, 'gy', 0, 0).astype(F32)  9.38 us
    dot_general x2, matrix products, product(): out = jnp.dot(left, weight, preferred_element_type=F32)  7.16 us
    ppermute x6, starting transfers between devices, shift_z(): return lax.ppermute(x, 'gx', [(i, (i + 2 * k) % 8) for i in range(8)])  6.98 us
  transfers between devices with their start and end apart: 9, of which 6 were waited for; matrix products, arithmetic and copies ran while one was open for 2% of the time, Pallas kernels for 0%

profile of v1, /device:TPU:1, one launch (start us, length us, event | category | flops | bytes accessed | tf_op | source)
XLA Modules:
  0.0 193.1 jit_solution(3988818913701553949)
XLA Ops:
  0.6 1.5 collective-permute-start
  2.1 0.8 subtract_convert_fusion.8
  2.9 0.8 subtract_convert_fusion.7
  3.7 0.8 subtract_convert_fusion.6
  4.4 0.8 subtract_convert_fusion.5
  5.3 0.7 select_bitcast_fusion.2
  6.0 3.9 %collective-permute-start.1 = (bf16[2,64,116]{2,1,0:T(8,128)(2,1)S(1)}, bf16[2,64,116]{2,1,0:T(8,128)(2,1)S(1)}, u32[]{:S(2)}, u32[]{:S(2)}) collective-permute-start(bf16[2,64,116]{2,1,0:T(8,128)(2,1)S(1)} %pad_maximum_fusion.3), channel_id=1, source_target_pairs={{0,96},{16,112},{32,0},{48,16},{64,32},{80,48},{96,64},{112,80},{1... | collective-permute-start | bytes 89096 | tf_op jit(solution)/shard_map/ppermute | solution.py:69
  10.0 0.1 collective-permute-start.2
  10.1 0.7 collective-permute-start.3
  10.7 0.2 collective-permute-done.1
  11.0 3.4 %collective-permute-done.2 = bf16[2,64,116]{2,1,0:T(8,128)(2,1)S(1)} collective-permute-done((bf16[2,64,116]{2,1,0:T(8,128)(2,1)S(1)}, bf16[2,64,116]{2,1,0:T(8,128)(2,1)S(1)}, u32[]{:S(2)}, u32[]{:S(2)}) %collective-permute-start.2) | collective-permute-done | bytes 29728 | tf_op jit(solution)/shard_map/ppermute | solution.py:69
  14.6 0.1 fusion.35
  14.7 0.2 copy.93
  14.9 0.1 reshape.460
  15.0 0.8 multiply_convert_fusion
  15.9 4.3 %fusion.71 = f32[68,3712]{1,0:T(8,128)S(1)} fusion(bf16[68,928]{1,0:T(8,128)(2,1)S(1)} %concatenate.63, bf16[928,3712]{1,0:T(8,128)(2,1)} %param.19), kind=kOutput, calls=%fused_computation.162 | convolution fusion | flops 468484096 | bytes 8025344 | tf_op jit(solution)/shard_map/dot_general | solution.py:106
  20.3 2.9 %fusion.72 = f32[68,1984]{1,0:T(8,128)S(1)} fusion(bf16[68,928]{1,0:T(8,128)(2,1)S(1)} %concatenate.65, bf16[928,1984]{1,0:T(8,128)(2,1)} %param.17), kind=kOutput, calls=%fused_computation.163 | convolution fusion | flops 250396672 | bytes 4348160 | tf_op jit(solution)/shard_map/dot_general | solution.py:106
  23.4 0.2 multiply_reduce_fusion
  23.6 0.1 reshape.452
  23.7 0.1 reshape.453
  24.1 0.1 copy.86
  24.3 0.1 broadcast_in_dim.20
  24.5 0.5 pad_maximum_fusion
  25.0 0.1 broadcast_in_dim.21
  25.1 0.3 pad_maximum_fusion.1
  25.4 1.9 concatenate.67
  27.3 6.8 %all-to-all-start = ((bf16[16,8,5760]{2,1,0:T(8,128)(2,1)}), bf16[16,8,5760]{2,1,0:T(8,128)(2,1)S(1)}, u32[]{:S(2)}, u32[]{:S(2)}) async-start(bf16[16,8,5760]{2,1,0:T(8,128)(2,1)} %concatenate.67), calls=%async_computation | async-start | bytes 2949120 | tf_op jit(solution)/shard_map/all_to_all | solution.py:120
  34.1 0.1 multiply_cosine_fusion.1
  34.2 0.1 iota_compare_fusion
  34.3 19.2 %all-to-all-done = bf16[16,8,5760]{2,1,0:T(8,128)(2,1)S(1)} async-done(((bf16[16,8,5760]{2,1,0:T(8,128)(2,1)}), bf16[16,8,5760]{2,1,0:T(8,128)(2,1)S(1)}, u32[]{:S(2)}, u32[]{:S(2)}) %all-to-all-start) | async-done | bytes 1474592 | tf_op jit(solution)/shard_map/all_to_all | solution.py:120
  53.5 9.4 %copy.76 = bf16[16,8,5760]{0,1,2:T(8,128)(2,1)} copy(bf16[16,8,5760]{2,1,0:T(8,128)(2,1)S(1)} %all-to-all-done) | data formatting | bytes 2949120 | tf_op jit(solution)/shard_map/all_to_all | solution.py:120
  62.9 13.3 %convert_element_type.391 = f32[16,8,5760]{0,1,2:T(8,128)} convert(bf16[16,8,5760]{0,1,2:T(8,128)(2,1)} %copy.76) | non-fusion elementwise | flops 737280 | bytes 4423680 | tf_op jit(solution)/shard_map/convert_element_type | solution.py:120
  76.2 36.1 %slice_add_fusion.1 = (f32[16,1,5760]{0,1,2:T(1,128)S(1)}, f32[16,1,5760]{0,1,2:T(1,128)S(1)}) fusion(f32[16,8,5760]{0,1,2:T(8,128)} %convert_element_type.391), kind=kLoop, calls=%fused_computation.9 | loop fusion | flops 184320 | bytes 2211840 | tf_op jit(solution)/shard_map/add | solution.py:131
  112.3 0.8 fusion.68
  113.2 0.9 fusion.53
  114.1 0.2 slice.199
  114.3 34.5 %fusion = f32[4,5696]{0,1:T(8,128)} fusion(f32[16,8,5760]{0,1,2:T(8,128)} %convert_element_type.391, f32[16,5696]{0,1:T(8,128)S(1)} %slice.199, f32[16,4]{0,1:T(4,128)S(1)} %subtract_bitcast_fusion), kind=kLoop, calls=%fused_computation.1 | loop fusion | flops 1070848 | bytes 1914112 | tf_op jit(solution)/shard_map/reduce_sum | solution.py:132
  148.8 2.7 %copy.77 = f32[4,5696]{1,0:T(4,128)S(1)} copy(f32[4,5696]{0,1:T(8,128)} %fusion) | data formatting | bytes 182272 | tf_op jit(solution)/shard_map/reduce_sum | solution.py:132
  151.5 0.9 slice_reduce_fusion
  152.3 0.1 multiply_add_fusion
  152.5 0.1 reshape.454
  152.6 0.3 fusion.29
  152.9 0.1 fusion.49
  153.1 0.1 fusion.36
  153.1 0.2 fusion.43
  153.4 4.0 %fusion.70 = (f32[4,29]{1,0:T(4,128)S(1)}, f32[4,29,4096]{2,1,0:T(8,128)S(1)}) fusion(bf16[4,1,4096,128]{3,2,1,0:T(8,128)(2,1)} %param.21, bf16[4,29,32]{2,1,0:T(8,128)(2,1)S(1)} %get-tuple-element.27, bf16[4,29,32]{2,1,0:T(8,128)(2,1)S(1)} %get-tuple-element.26, pred[4,4096]{1,0:T(4,128)(4,1)S(1)} %iota_compare_fusion), kind=kOutput, calls=%fused_computation.161 | convolution fusion | flops 62272396 | bytes 6126544 | tf_op jit(solution)/shard_map/rgqd,rgtd->rgqt/dot_general | solution.py:38
  157.4 0.6 fusion.7
  158.0 1.6 fusion.15
  159.6 0.1 reshape.457
  159.8 0.2 broadcast_in_dim.25
  160.0 14.5 %all_to_all.10 = bf16[16,4,5568]{2,1,0:T(4,128)(2,1)S(1)} all-to-all(bf16[16,4,5568]{2,1,0:T(4,128)(2,1)S(1)} %broadcast_in_dim.25), channel_id=1, replica_groups=mesh['gx'=8,'gy'=16] {'gy'}, dimensions={0} | all-to-all | bytes 1425408 | tf_op jit(solution)/shard_map/all_to_all | solution.py:145
  174.4 0.3 reshape.458
  174.8 5.2 %fusion.22 = f32[64,928]{1,0:T(8,128)S(1)} fusion(bf16[3712,928]{0,1:T(8,128)(2,1)} %param.20, bf16[64,5568]{1,0:T(8,128)(2,1)S(1)} %reshape.458), kind=kOutput, calls=%fused_computation.26 | convolution fusion | flops 440926208 | bytes 7602176 | tf_op jit(solution)/shard_map/dot_general | solution.py:146
  179.9 1.2 convolution_add_fusion
  181.1 0.6 reshape.459
  181.9 4.2 %collective-permute-start.4 = (f32[4,64,116]{2,1,0:T(8,128)S(1)}, f32[4,64,116]{2,1,0:T(8,128)S(1)}, u32[]{:S(2)}, u32[]{:S(2)}) collective-permute-start(f32[4,64,116]{2,1,0:T(8,128)S(1)} %select_bitcast_fusion), channel_id=1, source_target_pairs={{0,16},{16,0},{32,48},{48,32},{64,80},{80,64},{96,112},{112,96},{1... | collective-permute-start | bytes 356360 | tf_op jit(solution)/shard_map/ppermute | solution.py:65
  186.1 1.0 collective-permute-done.4
  187.2 0.8 collective-permute-start.7
  188.0 0.7 collective-permute-start.6
  188.7 0.8 collective-permute-start.5
  189.5 0.6 pad_maximum_fusion.9
  190.1 2.0 %collective-permute-done.6 = bf16[64,116]{1,0:T(8,128)(2,1)S(1)} collective-permute-done((bf16[64,116]{1,0:T(8,128)(2,1)S(1)}, bf16[64,116]{1,0:T(8,128)(2,1)S(1)}, u32[]{:S(2)}, u32[]{:S(2)}) %collective-permute-start.6) | collective-permute-done | bytes 14880 | tf_op jit(solution)/shard_map/ppermute | solution.py:69
  192.1 0.4 collective-permute-done.5
  192.5 0.6 fusion.42
  (67 shorter events, 1.4 us)
Async XLA Ops:
  0.6 4.7 %collective-permute-start = (bf16[64,116]{1,0:T(8,128)(2,1)}, bf16[64,116]{1,0:T(8,128)(2,1)S(1)}, u32[]{:S(2)}, u32[]{:S(2)}) collective-permute-start(bf16[64,116]{1,0:T(8,128)(2,1)} %param.11), channel_id=1, source_target_pairs={{0,16},{16,0},{32,48},{48,32},{64,80},{80,64},{96,112},{112,96},{1... | collective-permute-start | bytes 44552 | tf_op jit(solution)/shard_map/ppermute | solution.py:65
  6.0 4.9 %collective-permute-start.1 = (bf16[2,64,116]{2,1,0:T(8,128)(2,1)S(1)}, bf16[2,64,116]{2,1,0:T(8,128)(2,1)S(1)}, u32[]{:S(2)}, u32[]{:S(2)}) collective-permute-start(bf16[2,64,116]{2,1,0:T(8,128)(2,1)S(1)} %pad_maximum_fusion.3), channel_id=1, source_target_pairs={{0,96},{16,112},{32,0},{48,16},{64,32},{80,48},{96,64},{112,80},{1... | collective-permute-start | bytes 89096 | tf_op jit(solution)/shard_map/ppermute | solution.py:69
  10.0 4.5 %collective-permute-start.2 = (bf16[2,64,116]{2,1,0:T(8,128)(2,1)S(1)}, bf16[2,64,116]{2,1,0:T(8,128)(2,1)S(1)}, u32[]{:S(2)}, u32[]{:S(2)}) collective-permute-start(bf16[2,64,116]{2,1,0:T(8,128)(2,1)S(1)} %pad_maximum_fusion.3), channel_id=1, source_target_pairs={{0,64},{16,80},{32,96},{48,112},{64,0},{80,16},{96,32},{112,48},{1... | collective-permute-start | bytes 89096 | tf_op jit(solution)/shard_map/ppermute | solution.py:69
  10.1 4.4 %collective-permute-start.3 = (bf16[2,64,116]{2,1,0:T(8,128)(2,1)S(1)}, bf16[2,64,116]{2,1,0:T(8,128)(2,1)S(1)}, u32[]{:S(2)}, u32[]{:S(2)}) collective-permute-start(bf16[2,64,116]{2,1,0:T(8,128)(2,1)S(1)} %pad_maximum_fusion.3), channel_id=1, source_target_pairs={{0,32},{16,48},{32,64},{48,80},{64,96},{80,112},{96,0},{112,16},{1... | collective-permute-start | bytes 89096 | tf_op jit(solution)/shard_map/ppermute | solution.py:69
  25.4 8.7 %copy-start.3 = (s32[4]{0:T(128)S(1)}, s32[4]{0:T(128)}, u32[]{:S(2)}) copy-start(s32[4]{0:T(128)} %param.12) | copy-start | bytes 52
  27.3 26.2 %all-to-all-start = ((bf16[16,8,5760]{2,1,0:T(8,128)(2,1)}), bf16[16,8,5760]{2,1,0:T(8,128)(2,1)S(1)}, u32[]{:S(2)}, u32[]{:S(2)}) async-start(bf16[16,8,5760]{2,1,0:T(8,128)(2,1)} %concatenate.67), calls=%async_computation | async-start | bytes 2949120 | tf_op jit(solution)/shard_map/all_to_all | solution.py:120
  153.4 4.6 %copy-start = (bf16[4,1,4096,128]{3,2,1,0:T(8,128)(2,1)S(1)}, bf16[4,1,4096,128]{3,2,1,0:T(8,128)(2,1)}, u32[]{:S(2)}) copy-start(bf16[4,1,4096,128]{3,2,1,0:T(8,128)(2,1)} %param.21) | copy-start | bytes 12582916
  174.7 5.2 %copy-start.1 = (bf16[1856,928]{0,1:T(8,128)(2,1)S(1)}, bf16[1856,928]{0,1:T(8,128)(2,1)}, u32[]{:S(2)}) copy-start(bf16[1856,928]{0,1:T(8,128)(2,1)} %param.18) | copy-start | bytes 10334212
  179.9 12.6 %copy-start.2 = (bf16[64,116]{1,0:T(8,128)(2,1)S(1)}, bf16[64,116]{1,0:T(8,128)(2,1)}, u32[]{:S(2)}) copy-start(bf16[64,116]{1,0:T(8,128)(2,1)} %param.11) | copy-start | bytes 44548
  181.9 5.2 %collective-permute-start.4 = (f32[4,64,116]{2,1,0:T(8,128)S(1)}, f32[4,64,116]{2,1,0:T(8,128)S(1)}, u32[]{:S(2)}, u32[]{:S(2)}) collective-permute-start(f32[4,64,116]{2,1,0:T(8,128)S(1)} %select_bitcast_fusion), channel_id=1, source_target_pairs={{0,16},{16,0},{32,48},{48,32},{64,80},{80,64},{96,112},{112,96},{1... | collective-permute-start | bytes 356360 | tf_op jit(solution)/shard_map/ppermute | solution.py:65
  187.2 2.9 %collective-permute-start.7 = (bf16[64,116]{1,0:T(8,128)(2,1)S(1)}, bf16[64,116]{1,0:T(8,128)(2,1)S(1)}, u32[]{:S(2)}, u32[]{:S(2)}) collective-permute-start(bf16[64,116]{1,0:T(8,128)(2,1)S(1)} %get-tuple-element.29), channel_id=1, source_target_pairs={{0,96},{16,112},{32,0},{48,16},{64,32},{80,48},{96,64},{112,80},{1... | collective-permute-start | bytes 44552 | tf_op jit(solution)/shard_map/ppermute | solution.py:69
  188.0 4.1 %collective-permute-start.6 = (bf16[64,116]{1,0:T(8,128)(2,1)S(1)}, bf16[64,116]{1,0:T(8,128)(2,1)S(1)}, u32[]{:S(2)}, u32[]{:S(2)}) collective-permute-start(bf16[64,116]{1,0:T(8,128)(2,1)S(1)} %get-tuple-element.30), channel_id=1, source_target_pairs={{0,64},{16,80},{32,96},{48,112},{64,0},{80,16},{96,32},{112,48},{1... | collective-permute-start | bytes 44552 | tf_op jit(solution)/shard_map/ppermute | solution.py:69
  188.7 3.8 %collective-permute-start.5 = (bf16[64,116]{1,0:T(8,128)(2,1)S(1)}, bf16[64,116]{1,0:T(8,128)(2,1)S(1)}, u32[]{:S(2)}, u32[]{:S(2)}) collective-permute-start(bf16[64,116]{1,0:T(8,128)(2,1)S(1)} %get-tuple-element.28), channel_id=1, source_target_pairs={{0,32},{16,48},{32,64},{48,80},{64,96},{80,112},{96,0},{112,16},{1... | collective-permute-start | bytes 44552 | tf_op jit(solution)/shard_map/ppermute | solution.py:69

commit v2 on v0

v2 whole, which is shorter than its diff:
```python
import functools
import math

import jax
import jax.numpy as jnp
import numpy as np
from jax import lax
from jax.experimental import pallas as pl
from jax.experimental.pallas import tpu as pltpu
from jax.sharding import PartitionSpec as P

HD = 64
QPG = 29
EPS = 1e-05
THETA = 10000.0
BF = jnp.bfloat16
F32 = jnp.float32
LANES = 128
GY = 16
OWN = 4
ROWS = GY * OWN
BLOCK = 256
QKV_BLOCKS = 8
AT_SIDE = ROWS
AT_QKV = AT_SIDE + 8
AT_GAIN = AT_QKV + OWN * QKV_BLOCKS
AT_BIAS = AT_GAIN + QKV_BLOCKS
PAYLOAD = AT_BIAS + QKV_BLOCKS
RESULT = ROWS + OWN * QKV_BLOCKS
VM = pl.BlockSpec(memory_space=pltpu.VMEM)
SM = pl.BlockSpec(memory_space=pltpu.SMEM)
HB = pl.BlockSpec(memory_space=pl.ANY)
PARAMS = pltpu.CompilerParams(vmem_limit_bytes=16 << 20)


def in_vmem(x):
    return pltpu.with_memory_space_constraint(x, pltpu.VMEM)


def swap_core(x):
    return lax.ppermute(x, "gx", [(i, i ^ 1) for i in range(8)])


def shift_z(x, k):
    return lax.ppermute(x, "gx", [(i, (i + 2 * k) % 8) for i in range(8)])


def chunks(total, step):
    return [(at, min(step, total - at)) for at in range(0, total, step)]


def place():
    at = lax.axis_index("gx")
    return lax.div(at, 2), lax.rem(at, 2)


def three(value):
    out = []
    for _ in range(3):
        part = value.astype(BF).astype(F32)
        out.append(part)
        value = value - part
    return out


def product_kernel(g0, g1, g2, g3, gm, bm, ga, ba, w_up, w_qkv, out, blocks, flat, spread, side):
    z, core = place()
    narrow = g0.shape[2]
    wide = 8 * narrow
    for k, g in enumerate((g0, g1, g2, g3)):
        at = lax.rem(z + 4 - k, 4)
        blocks[2 * at + core] = g[0]
        blocks[2 * at + 1 - core] = g[1]
    for i in range(8):
        flat[:, narrow * i : narrow * (i + 1)] = blocks[i].astype(F32)
    values = flat[...]
    part_sum = jnp.sum(values, axis=1, keepdims=True)
    shifted = values - part_sum * (1.0 / wide)
    part_square = jnp.sum(shifted * shifted, axis=1, keepdims=True)
    up_cols, qkv_cols = w_up.shape[1], w_qkv.shape[1]

    lane = lax.broadcasted_iota(jnp.int32, (ROWS, LANES), 1)
    stats = jnp.zeros(lane.shape, F32)
    for i, part in enumerate(three(part_sum) + three(part_square)):
        stats = jnp.where(lane == 2 + i, part, stats)
    stats = jnp.transpose(stats)[:8]
    stats = jnp.concatenate([stats, jnp.zeros((8, BLOCK - ROWS), F32)], axis=1)
    row = lax.broadcasted_iota(jnp.int32, (8, 1), 0)

    def left(gain, bias):
        lower = jnp.where(row == 0, gain[...], jnp.where(row == 1, bias[...], 0.0))
        return jnp.concatenate([shifted * gain[...], lower], axis=0).astype(BF)

    left_m = left(gm, bm)
    for at, size in chunks(up_cols, 2 * BLOCK):
        got = jnp.dot(left_m, w_up[:, at : at + size], preferred_element_type=F32)
        if size < 2 * BLOCK:
            got = jnp.concatenate([got, jnp.zeros((ROWS + 8, 2 * BLOCK - size), F32)], axis=1)
        for j in range(2):
            p = at // BLOCK + j
            part = got[:, j * BLOCK : (j + 1) * BLOCK]
            out[p, :ROWS, :] = part[:ROWS].astype(BF)
            out[p, AT_SIDE:AT_QKV, :] = jnp.where(row < 2, part[ROWS:], stats).astype(BF)
    left_a = left(ga, ba)
    for at, size in chunks(qkv_cols, 2 * BLOCK):
        got = jnp.dot(left_a, w_qkv[:, at : at + size], preferred_element_type=F32)
        if size < 2 * BLOCK:
            got = jnp.concatenate([got, jnp.zeros((ROWS + 8, 2 * BLOCK - size), F32)], axis=1)
        for j in range(2):
            b = at // BLOCK + j
            part = got[:, j * BLOCK : (j + 1) * BLOCK]
            for h in range(2):
                cols = slice(h * LANES, (h + 1) * LANES)
                spread[h, pl.ds(b, ROWS, stride=QKV_BLOCKS), :] = part[:ROWS, cols]
            side[b : b + 1, :] = part[ROWS : ROWS + 1]
            side[QKV_BLOCKS + b : QKV_BLOCKS + b + 1, :] = part[ROWS + 1 : ROWS + 2]
    both = side[...].astype(BF)
    step = OWN * QKV_BLOCKS
    for p in range(GY):
        for h in range(2):
            cols = slice(h * LANES, (h + 1) * LANES)
            out[p, AT_QKV:AT_GAIN, cols] = spread[h, p * step : (p + 1) * step, :].astype(BF)
        out[p, AT_GAIN:, :] = both


def middle_kernel(wide, lengths, got, inverse, cache, block, new_kv, columns):
    width = wide * GY
    own_at = lax.axis_index("gy") * OWN

    sums, squares = [], []
    for d in range(GY):
        stat = got[d, AT_SIDE:AT_QKV, :LANES].astype(F32)
        sums.append(stat[2:3] + stat[3:4] + stat[4:5])
        squares.append(stat[5:6] + stat[6:7] + stat[7:8])
    mean = functools.reduce(jnp.add, sums) * (1.0 / width)
    gaps = [s * (1.0 / wide) - mean for s in sums]
    var = functools.reduce(jnp.add, [q + wide * g * g for q, g in zip(squares, gaps)]) * (1.0 / width)
    scale = 1.0 / jnp.sqrt(var + EPS)
    table = jnp.concatenate(gaps + [scale, jnp.zeros((LANES - GY - 1, LANES), F32)], axis=0)
    columns[...] = jnp.transpose(table)
    whole = columns[:ROWS]

    acc = jnp.zeros((ROWS, BLOCK), F32)
    plain = jnp.zeros((1, BLOCK), F32)
    for d in range(GY):
        side = got[d, AT_SIDE:AT_QKV, :].astype(F32)
        acc = acc + (got[d, :ROWS, :].astype(F32) + whole[:, d : d + 1] * side[0:1])
        plain = plain + side[1:2]
    up = whole[:, GY : GY + 1] * acc + plain
    hidden = 0.5 * up * (1.0 + lax.erf(up * math.sqrt(0.5)))
    block[:ROWS, :] = hidden.astype(BF)

    plain = jnp.zeros((QKV_BLOCKS, BLOCK), F32)
    for d in range(GY):
        plain = plain + got[d, AT_BIAS:, :].astype(F32)
    lane = lax.broadcasted_iota(jnp.int32, (1, LANES), 1)
    first = lane < HD
    half = lane % HD < HD // 2
    length = cache.shape[2]
    position = lax.broadcasted_iota(jnp.int32, (1, length), 1)
    factor = 1.0 / math.sqrt(HD)
    for r in range(OWN):
        mine = columns[pl.ds(own_at + r, 1), :]
        acc = jnp.zeros((QKV_BLOCKS, BLOCK), F32)
        for d in range(GY):
            lo = AT_QKV + QKV_BLOCKS * r
            part = got[d, lo : lo + QKV_BLOCKS, :].astype(F32)
            acc = acc + (part + mine[:, d : d + 1] * got[d, AT_GAIN:AT_BIAS, :].astype(F32))
        qkv = (mine[:, GY : GY + 1] * acc + plain).astype(BF).astype(F32)
        angle = lengths[r].astype(F32) * inverse[...]
        cosine = jnp.cos(angle)
        sine = jnp.sin(angle)
        sine = jnp.where(half, -sine, sine)
        pieces = []
        for h in range(2):
            pairs = qkv[:, h * LANES : (h + 1) * LANES]
            other = jnp.where(
                half, pltpu.roll(pairs, LANES - HD // 2, 1), pltpu.roll(pairs, HD // 2, 1)
            )
            turned = (pairs * cosine + other * sine).astype(BF).astype(F32)
            pieces.append(jnp.where(first, turned, 0.0))
            pieces.append(jnp.where(first, pltpu.roll(turned, HD, 1), 0.0))
        query = jnp.concatenate(pieces, axis=0)
        key = query[15:16]
        value = jnp.where(first, 0.0, pltpu.roll(qkv[7:8, LANES:], HD, 1))
        new_kv[r] = (key + value).astype(BF)
        keys = cache[r, 0]
        scores = lax.dot_general(
            query.astype(BF), keys, (((1,), (1,)), ((), ())), preferred_element_type=F32
        )
        scores = scores * factor
        live = position < lengths[r]
        scores = jnp.where(live, scores, -1e30)
        own = jnp.sum(query * key, axis=1, keepdims=True) * factor
        top = jnp.maximum(jnp.max(scores, axis=1, keepdims=True), own)
        probs = jnp.where(live, jnp.exp(scores - top), 0.0)
        own_prob = jnp.exp(own - top)
        total = jnp.sum(probs, axis=1, keepdims=True) + own_prob
        summed = jnp.dot(probs.astype(BF), keys, preferred_element_type=F32)
        summed = summed + own_prob.astype(BF).astype(F32) * value
        result = summed / total
        lo = ROWS + QKV_BLOCKS * r
        for h in range(2):
            even, odd = result[16 * h : 16 * h + 8], result[16 * h + 8 : 16 * h + 16]
            pairs = jnp.where(first, pltpu.roll(even, HD, 1), odd)
            block[lo : lo + QKV_BLOCKS, h * LANES : (h + 1) * LANES] = pairs.astype(BF)


def last_kernel(every, w_down, w_out, keep, send, spread, blocks):
    z, core = place()
    up_cols, attn_cols = w_down.shape[1], w_out.shape[1]
    narrow = keep.shape[2]
    both = (((1,), (1,)), ((), ()))
    step = OWN * QKV_BLOCKS
    for d in range(GY):
        for h in range(2):
            cols = slice(h * LANES, (h + 1) * LANES)
            spread[h, d * step : (d + 1) * step, :] = every[d, ROWS:, cols].astype(F32)
    part = jnp.zeros((ROWS, w_down.shape[0]), F32)
    for d, (at, size) in enumerate(chunks(up_cols, BLOCK)):
        part = part + lax.dot_general(
            every[d, :ROWS, :size], w_down[:, at : at + size], both, preferred_element_type=F32
        )
    for b, (at, size) in enumerate(chunks(attn_cols, BLOCK)):
        left = [spread[h, pl.ds(b, ROWS, stride=QKV_BLOCKS), :].astype(BF) for h in range(2)]
        left = jnp.concatenate(left, axis=1)
        part = part + lax.dot_general(
            left[:, :size], w_out[:, at : at + size], both, preferred_element_type=F32
        )
    for i in range(8):
        blocks[i] = part[:, narrow * i : narrow * (i + 1)]
    for k in range(4):
        at = lax.rem(z + k, 4)
        keep[k] = blocks[2 * at + core]
        send[k] = blocks[2 * at + 1 - core]


def local(
    tokens, lengths, gain_attn, bias_attn, gain_mlp, bias_mlp, w_qkv, w_out, w_up, w_down, cache
):
    rows, narrow = tokens.shape
    wide = gain_attn.shape[0]

    pair = jnp.stack([tokens, swap_core(tokens)])
    got = [pair] + [shift_z(pair, k) for k in (1, 2, 3)]
    vectors = [v.reshape(1, wide) for v in (gain_mlp, bias_mlp, gain_attn, bias_attn)]
    payload = pl.pallas_call(
        product_kernel,
        out_shape=jax.ShapeDtypeStruct((GY, PAYLOAD, BLOCK), BF),
        in_specs=[VM] * 10,
        out_specs=VM,
        scratch_shapes=[
            pltpu.VMEM((8, rows, narrow), BF),
            pltpu.VMEM((rows, wide), F32),
            pltpu.VMEM((2, rows * QKV_BLOCKS, LANES), F32),
            pltpu.VMEM((2 * QKV_BLOCKS, BLOCK), F32),
        ],
        compiler_params=PARAMS,
        name="product",
    )(*got, *vectors, in_vmem(w_up), in_vmem(w_qkv))

    steps = np.arange(HD // 2, dtype=np.float64) * (2.0 / HD)
    inverse = jnp.asarray(np.tile(np.power(THETA, -steps), 4)[None].astype(np.float32))
    summed = lax.all_to_all(payload, "gy", 0, 0)
    block, new_kv = pl.pallas_call(
        functools.partial(middle_kernel, wide),
        out_shape=(
            jax.ShapeDtypeStruct((RESULT, BLOCK), BF),
            jax.ShapeDtypeStruct((OWN, 1, 2 * HD), BF),
        ),
        in_specs=[SM] + [VM] * 3,
        out_specs=(VM, VM),
        scratch_shapes=[pltpu.VMEM((LANES, LANES), F32)],
        compiler_params=PARAMS,
        name="middle",
    )(lengths, summed, inverse, in_vmem(cache))

    every = lax.all_to_all(jnp.broadcast_to(block[None], (GY, RESULT, BLOCK)), "gy", 0, 0)
    half = jax.ShapeDtypeStruct((4, rows, narrow), F32)
    keep, send = pl.pallas_call(
        last_kernel,
        out_shape=(half, half),
        in_specs=[VM] * 3,
        out_specs=(VM, VM),
        scratch_shapes=[
            pltpu.VMEM((2, rows * QKV_BLOCKS, LANES), F32),
            pltpu.VMEM((8, rows, narrow), F32),
        ],
        compiler_params=PARAMS,
        name="last",
    )(every, in_vmem(w_down.T), in_vmem(w_out.T))

    keep = keep + swap_core(send)
    narrowed = keep.astype(BF)
    total = keep[0]
    for k in (1, 2, 3):
        total = total + shift_z(narrowed[k], k).astype(F32)
    mixed = (tokens.astype(F32) + total).astype(BF)
    return (mixed, new_kv)


def solution(mesh):
    in_specs = (
        P(None, ("gy", "gx")),
        P("gy"),
        P("gy"),
        P("gy"),
        P("gy"),
        P("gy"),
        P("gy", "gx"),
        P("gx", "gy"),
        P("gy", "gx"),
        P("gx", "gy"),
        P("gy", "gx", None, None),
    )
    out_specs = (P(None, ("gy", "gx")), P("gy", "gx", None))
    return jax.shard_map(local, mesh=mesh, in_specs=in_specs, out_specs=out_specs, check_vma=False)
```

time: 329 us -> 78.8 us (0.24)
  waiting for transfers between devices: 146 us -> 9.19 us
  blocking collectives: 129 us -> 34.5 us
  matrix products: 23.4 us -> 0 us
  between operations: 16.2 us -> 0.71 us
  starting transfers between devices: 0.08 us -> 13.6 us
  Pallas kernels: 0 us -> 9.92 us
  other arithmetic: 5.89 us -> 1.37 us
    unnamed x4 -> x0, waiting for transfers between devices: 146 us -> none
    psum x1 -> x0, blocking collectives: 68.7 us -> none  [local(): lax.psum((jnp.sum(values, axis=1), jnp.sum(values * values, axis=1)), ('g...]
    all_gather x4 -> x0, blocking collectives: 60.1 us -> none  [the longest x1 17.2 us: local(): lax.all_gather(attn, 'gy', axis=0, tiled=True)]
    all_to_all x0 -> x2, blocking collectives: none -> 34.5 us  [the longest x1 21 us: local(): summed = lax.all_to_all(payload, 'gy', 0, 0)]
    dot_general x7 -> x0, matrix products: 23.4 us -> none  [the longest x1 5.67 us: local(): jnp.dot(lax.all_gather(hidden, 'gy', axis=1, tiled=True), w_down, preferr...]
    ppermute x0 -> x8, starting transfers between devices: none -> 13.6 us  [the longest x6 7.35 us: shift_z(): return lax.ppermute(x, 'gx', [(i, (i + 2 * k) % 8) for i in range(8)])]
    pallas_call x0 -> x3, Pallas kernels: none -> 9.92 us  [the longest x1 4.46 us: local(): pl.pallas_call(functools.partial(middle_kernel, wide), out_shape=(jax.Sha...]
    ppermute x0 -> x8, waiting for transfers between devices: none -> 9.19 us  [the longest x6 7.15 us: shift_z(): return lax.ppermute(x, 'gx', [(i, (i + 2 * k) % 8) for i in range(8)])]
  transfers between devices with their start and end apart: 2 -> 8, of which waited for: 2 -> 6; matrix products, arithmetic and copies ran while one was open for 1% -> 1% of each run, Pallas kernels for 0% -> 0%
where the time goes in v2:
time: 78.8 us; the launch traced here: 77.7 us
  blocking collectives  34.5 us (44%)
  starting transfers between devices  13.6 us (17%)
  Pallas kernels  9.92 us (13%)
  waiting for transfers between devices  9.19 us (12%)
  local copies, waits for them, and re-layouts  8.45 us (11%)
  other arithmetic  1.37 us (2%)
    all_to_all x1, blocking collectives, local(): summed = lax.all_to_all(payload, 'gy', 0, 0)  21 us
    all_to_all x1, blocking collectives, local(): lax.all_to_all(jnp.broadcast_to(block[None], (GY, RESULT, BLOCK)), 'gy',...  13.5 us
    unnamed x25, local copies, waits for them, and re-layouts  8.37 us
    ppermute x6, starting transfers between devices, shift_z(): return lax.ppermute(x, 'gx', [(i, (i + 2 * k) % 8) for i in range(8)])  7.35 us
    ppermute x6, waiting for transfers between devices, shift_z(): return lax.ppermute(x, 'gx', [(i, (i + 2 * k) % 8) for i in range(8)])  7.15 us
    ppermute x2, starting transfers between devices, swap_core(): return lax.ppermute(x, 'gx', [(i, i ^ 1) for i in range(8)])  6.24 us
    pallas_call x1, Pallas kernels, local(): pl.pallas_call(functools.partial(middle_kernel, wide), out_shape=(jax.Sha...  4.46 us
    pallas_call x1, Pallas kernels, local(): pl.pallas_call(last_kernel, out_shape=(half, half), in_specs=[VM] * 3, ou...  3.23 us
  transfers between devices with their start and end apart: 8, of which 6 were waited for; matrix products, arithmetic and copies ran while one was open for 1% of the time, Pallas kernels for 0%

profile of v2, /device:TPU:1, one launch (start us, length us, event | category | flops | bytes accessed | tf_op | source)
XLA Modules:
  0.0 77.7 jit_solution(8718257409465446984)
XLA Ops:
  0.6 1.5 %collective-permute-start = (bf16[64,116]{1,0:T(8,128)(2,1)}, bf16[64,116]{1,0:T(8,128)(2,1)S(1)}, u32[]{:S(2)}, u32[]{:S(2)}) collective-permute-start(bf16[64,116]{1,0:T(8,128)(2,1)} %param.12), channel_id=1, source_target_pairs={{0,16},{16,0},{32,48},{48,32},{64,80},{80,64},{96,112},{112,96},{1... | collective-permute-start | bytes 44552 | tf_op jit(solution)/shard_map/ppermute | solution.py:41
  2.1 1.0 %collective-permute-done = bf16[64,116]{1,0:T(8,128)(2,1)S(1)} collective-permute-done((bf16[64,116]{1,0:T(8,128)(2,1)}, bf16[64,116]{1,0:T(8,128)(2,1)S(1)}, u32[]{:S(2)}, u32[]{:S(2)}) %collective-permute-start) | collective-permute-done | bytes 14880 | tf_op jit(solution)/shard_map/ppermute | solution.py:41
  3.2 0.7 pad_maximum_fusion.g0
  3.9 3.9 %collective-permute-start.3 = (bf16[2,64,116]{2,1,0:T(8,128)(2,1)S(1)}, bf16[2,64,116]{2,1,0:T(8,128)(2,1)S(1)}, u32[]{:S(2)}, u32[]{:S(2)}) collective-permute-start(bf16[2,64,116]{2,1,0:T(8,128)(2,1)S(1)} %pad_maximum_fusion.g0), channel_id=1, source_target_pairs={{0,96},{16,112},{32,0},{48,16},{64,32},{80,48},{96,64},{112,80},{1... | collective-permute-start | bytes 89096 | tf_op jit(solution)/shard_map/ppermute | solution.py:45
  7.8 0.0 collective-permute-start.2
  7.8 0.7 collective-permute-start.1
  8.5 0.3 collective-permute-done.3.g3
  8.8 3.3 %collective-permute-done.2.g2 = bf16[2,64,116]{2,1,0:T(8,128)(2,1)S(1)} collective-permute-done((bf16[2,64,116]{2,1,0:T(8,128)(2,1)S(1)}, bf16[2,64,116]{2,1,0:T(8,128)(2,1)S(1)}, u32[]{:S(2)}, u32[]{:S(2)}) %collective-permute-start.2) | collective-permute-done | bytes 29728 | tf_op jit(solution)/shard_map/ppermute | solution.py:45
  12.1 0.0 collective-permute-done.1.g1
  12.2 0.0 copy-start
  12.2 3.0 %copy-done = bf16[928,3712]{1,0:T(8,128)(2,1)S(1)} copy-done((bf16[928,3712]{1,0:T(8,128)(2,1)S(1)}, bf16[928,3712]{1,0:T(8,128)(2,1)}, u32[]{:S(2)}) %copy-start) | copy-done | bytes 6889496
  15.1 0.0 copy-start.3
  15.1 2.1 %copy-done.3 = bf16[928,1984]{1,0:T(8,128)(2,1)S(1)} copy-done((bf16[928,1984]{1,0:T(8,128)(2,1)S(1)}, bf16[928,1984]{1,0:T(8,128)(2,1)}, u32[]{:S(2)}) %copy-start.3) | copy-done | bytes 3682328
  17.2 0.0 copy-start.5
  17.2 0.7 copy-done.5
  17.9 0.0 copy-start.6
  17.9 0.7 copy-done.6
  18.6 0.0 copy-start.7
  18.6 0.7 copy-done.7
  19.2 0.0 copy-start.8
  19.2 0.7 copy-done.8
  19.9 0.0 copy-start.2
  19.9 0.0 copy-start.9
  19.9 0.0 copy-start.10
  19.9 0.0 copy-start.4
  19.9 2.2 %product.1 = bf16[16,120,256]{2,1,0:T(8,128)(2,1)S(1)} custom-call(bf16[2,64,116]{2,1,0:T(8,128)(2,1)S(1)} %pad_maximum_fusion.g0, bf16[2,64,116]{2,1,0:T(8,128)(2,1)S(1)} %collective-permute-done.1.g1, bf16[2,64,116]{2,1,0:T(8,128)(2,1)S(1)} %collective-permute-done.2.g2, bf16[2,64,116]{2,1,0:T(8,128)(2,1)S(1)} %collective-permute-done.3.g3, ...), custom_call_target="tpu_custom_call" | custom-call | tf_op jit(solution)/shard_map/product/pallas_call | solution.py:247
  22.2 21.0 %all_to_all.10.got = bf16[16,120,256]{2,1,0:T(8,128)(2,1)S(1)} all-to-all(bf16[16,120,256]{2,1,0:T(8,128)(2,1)S(1)} %product.1), channel_id=1, replica_groups=mesh['gx'=8,'gy'=16] {'gy'}, dimensions={0} | all-to-all | bytes 1966080 | tf_op jit(solution)/shard_map/all_to_all | solution.py:264
  43.2 0.0 copy-done.2
  43.2 0.0 copy-done.9
  43.2 0.0 copy-done.10
  43.2 0.0 copy-start.1
  43.2 4.5 %middle.1 = (bf16[96,256]{1,0:T(8,128)(2,1)S(1)}, bf16[4,1,128]{2,1,0:T(2,128)(2,1)S(1)}) custom-call(s32[4]{0:T(128)S(1)} %copy-done.9, bf16[16,120,256]{2,1,0:T(8,128)(2,1)S(1)} %all_to_all.10.got, f32[1,128]{1,0:T(1,128)S(1)} %copy-done.10, bf16[4,1,4096,128]{3,2,1,0:T(8,128)(2,1)S(1)} %copy-done.2), custom_call_target="tpu_custom_call" | custom-call | tf_op jit(solution)/shard_map/middle/pallas_call | solution.py:265
  47.7 0.1 broadcast_in_dim.2
  47.8 13.5 %all_to_all.11.every = bf16[16,96,256]{2,1,0:T(8,128)(2,1)S(1)} all-to-all(bf16[16,96,256]{2,1,0:T(8,128)(2,1)S(1)} %broadcast_in_dim.2), channel_id=1, replica_groups=mesh['gx'=8,'gy'=16] {'gy'}, dimensions={0} | all-to-all | bytes 1572864 | tf_op jit(solution)/shard_map/all_to_all | solution.py:278
  61.3 0.0 copy-done.4
  61.3 0.0 copy-done.1
  61.3 0.0 copy-start.11
  61.3 3.2 %last.1 = (f32[4,64,116]{2,1,0:T(8,128)S(1)}, f32[4,64,116]{2,1,0:T(8,128)S(1)}) custom-call(bf16[16,96,256]{2,1,0:T(8,128)(2,1)S(1)} %all_to_all.11.every, bf16[928,3712]{1,0:T(8,128)(2,1)S(1)} %bitcast.26, bf16[928,1856]{1,0:T(8,128)(2,1)S(1)} %bitcast.27), custom_call_target="tpu_custom_call" | custom-call | tf_op jit(solution)/shard_map/last/pallas_call | solution.py:280
  64.5 4.7 %collective-permute-start.4 = (f32[4,64,116]{2,1,0:T(8,128)S(1)}, f32[4,64,116]{2,1,0:T(8,128)S(1)}, u32[]{:S(2)}, u32[]{:S(2)}) collective-permute-start(f32[4,64,116]{2,1,0:T(8,128)S(1)} %get-tuple-element.8), channel_id=1, source_target_pairs={{0,16},{16,0},{32,48},{48,32},{64,80},{80,64},{96,112},{112,96},{1... | collective-permute-start | bytes 356360 | tf_op jit(solution)/shard_map/ppermute | solution.py:41
  69.2 1.0 %collective-permute-done.4 = f32[4,64,116]{2,1,0:T(8,128)S(1)} collective-permute-done((f32[4,64,116]{2,1,0:T(8,128)S(1)}, f32[4,64,116]{2,1,0:T(8,128)S(1)}, u32[]{:S(2)}, u32[]{:S(2)}) %collective-permute-start.4) | collective-permute-done | bytes 118816 | tf_op jit(solution)/shard_map/ppermute | solution.py:41
  70.3 0.1 collective-permute-start.5
  70.4 2.7 %collective-permute-start.7 = (bf16[64,116]{1,0:T(8,128)(2,1)S(1)}, bf16[64,116]{1,0:T(8,128)(2,1)S(1)}, u32[]{:S(2)}, u32[]{:S(2)}) collective-permute-start(bf16[64,116]{1,0:T(8,128)(2,1)S(1)} %get-tuple-element.15), channel_id=1, source_target_pairs={{0,96},{16,112},{32,0},{48,16},{64,32},{80,48},{96,64},{112,80},{1... | collective-permute-start | bytes 44552 | tf_op jit(solution)/shard_map/ppermute | solution.py:45
  73.0 0.0 collective-permute-start.6
  73.0 0.6 copy.14
  73.6 0.6 collective-permute-done.5
  74.1 0.0 collective-permute-done.7
  74.1 3.0 %collective-permute-done.6 = bf16[64,116]{1,0:T(8,128)(2,1)S(1)} collective-permute-done((bf16[64,116]{1,0:T(8,128)(2,1)S(1)}, bf16[64,116]{1,0:T(8,128)(2,1)S(1)}, u32[]{:S(2)}, u32[]{:S(2)}) %collective-permute-start.6) | collective-permute-done | bytes 14880 | tf_op jit(solution)/shard_map/ppermute | solution.py:45
  77.1 0.0 copy-done.11
  77.1 0.6 fusion.4
  (2 shorter events, 0.0 us)
Async XLA Ops:
  0.6 2.6 %collective-permute-start = (bf16[64,116]{1,0:T(8,128)(2,1)}, bf16[64,116]{1,0:T(8,128)(2,1)S(1)}, u32[]{:S(2)}, u32[]{:S(2)}) collective-permute-start(bf16[64,116]{1,0:T(8,128)(2,1)} %param.12), channel_id=1, source_target_pairs={{0,16},{16,0},{32,48},{48,32},{64,80},{80,64},{96,112},{112,96},{1... | collective-permute-start | bytes 44552 | tf_op jit(solution)/shard_map/ppermute | solution.py:41
  3.9 4.9 %collective-permute-start.3 = (bf16[2,64,116]{2,1,0:T(8,128)(2,1)S(1)}, bf16[2,64,116]{2,1,0:T(8,128)(2,1)S(1)}, u32[]{:S(2)}, u32[]{:S(2)}) collective-permute-start(bf16[2,64,116]{2,1,0:T(8,128)(2,1)S(1)} %pad_maximum_fusion.g0), channel_id=1, source_target_pairs={{0,96},{16,112},{32,0},{48,16},{64,32},{80,48},{96,64},{112,80},{1... | collective-permute-start | bytes 89096 | tf_op jit(solution)/shard_map/ppermute | solution.py:45
  7.8 4.3 %collective-permute-start.2 = (bf16[2,64,116]{2,1,0:T(8,128)(2,1)S(1)}, bf16[2,64,116]{2,1,0:T(8,128)(2,1)S(1)}, u32[]{:S(2)}, u32[]{:S(2)}) collective-permute-start(bf16[2,64,116]{2,1,0:T(8,128)(2,1)S(1)} %pad_maximum_fusion.g0), channel_id=1, source_target_pairs={{0,64},{16,80},{32,96},{48,112},{64,0},{80,16},{96,32},{112,48},{1... | collective-permute-start | bytes 89096 | tf_op jit(solution)/shard_map/ppermute | solution.py:45
  7.8 4.3 %collective-permute-start.1 = (bf16[2,64,116]{2,1,0:T(8,128)(2,1)S(1)}, bf16[2,64,116]{2,1,0:T(8,128)(2,1)S(1)}, u32[]{:S(2)}, u32[]{:S(2)}) collective-permute-start(bf16[2,64,116]{2,1,0:T(8,128)(2,1)S(1)} %pad_maximum_fusion.g0), channel_id=1, source_target_pairs={{0,32},{16,48},{32,64},{48,80},{64,96},{80,112},{96,0},{112,16},{1... | collective-permute-start | bytes 89096 | tf_op jit(solution)/shard_map/ppermute | solution.py:45
  12.2 3.0 %copy-start = (bf16[928,3712]{1,0:T(8,128)(2,1)S(1)}, bf16[928,3712]{1,0:T(8,128)(2,1)}, u32[]{:S(2)}) copy-start(bf16[928,3712]{1,0:T(8,128)(2,1)} %w_up.1) | copy-start | bytes 20668420
  15.1 2.1 %copy-start.3 = (bf16[928,1984]{1,0:T(8,128)(2,1)S(1)}, bf16[928,1984]{1,0:T(8,128)(2,1)}, u32[]{:S(2)}) copy-start(bf16[928,1984]{1,0:T(8,128)(2,1)} %w_qkv.1) | copy-start | bytes 11046916
  17.2 0.7 copy-start.5
  17.9 0.7 copy-start.6
  18.6 0.7 copy-start.7
  19.2 0.7 copy-start.8
  19.9 23.3 %copy-start.2 = (bf16[4,1,4096,128]{3,2,1,0:T(8,128)(2,1)S(1)}, bf16[4,1,4096,128]{3,2,1,0:T(8,128)(2,1)}, u32[]{:S(2)}) copy-start(bf16[4,1,4096,128]{3,2,1,0:T(8,128)(2,1)} %cache.1) | copy-start | bytes 12582916
  19.9 23.3 %copy-start.9 = (s32[4]{0:T(128)S(1)}, s32[4]{0:T(128)}, u32[]{:S(2)}) copy-start(s32[4]{0:T(128)} %lengths.1) | copy-start | bytes 52
  19.9 23.3 %copy-start.10 = (f32[1,128]{1,0:T(1,128)S(1)}, f32[1,128]{1,0:T(1,128)}, u32[]{:S(2)}) copy-start(f32[1,128]{1,0:T(1,128)} %constant.2.clone.inverse) | copy-start | bytes 1540
  19.9 41.3 %copy-start.4 = (bf16[1856,928]{0,1:T(8,128)(2,1)S(1)}, bf16[1856,928]{0,1:T(8,128)(2,1)}, u32[]{:S(2)}) copy-start(bf16[1856,928]{0,1:T(8,128)(2,1)} %param.19) | copy-start | bytes 10334212
  43.2 18.1 %copy-start.1 = (bf16[3712,928]{0,1:T(8,128)(2,1)S(1)}, bf16[3712,928]{0,1:T(8,128)(2,1)}, u32[]{:S(2)}) copy-start(bf16[3712,928]{0,1:T(8,128)(2,1)} %param.21) | copy-start | bytes 20668420
  61.3 15.8 %copy-start.11 = (bf16[64,116]{1,0:T(8,128)(2,1)S(1)}, bf16[64,116]{1,0:T(8,128)(2,1)}, u32[]{:S(2)}) copy-start(bf16[64,116]{1,0:T(8,128)(2,1)} %param.12) | copy-start | bytes 44548
  64.5 5.7 %collective-permute-start.4 = (f32[4,64,116]{2,1,0:T(8,128)S(1)}, f32[4,64,116]{2,1,0:T(8,128)S(1)}, u32[]{:S(2)}, u32[]{:S(2)}) collective-permute-start(f32[4,64,116]{2,1,0:T(8,128)S(1)} %get-tuple-element.8), channel_id=1, source_target_pairs={{0,16},{16,0},{32,48},{48,32},{64,80},{80,64},{96,112},{112,96},{1... | collective-permute-start | bytes 356360 | tf_op jit(solution)/shard_map/ppermute | solution.py:41
  70.3 3.9 %collective-permute-start.5 = (bf16[64,116]{1,0:T(8,128)(2,1)S(1)}, bf16[64,116]{1,0:T(8,128)(2,1)S(1)}, u32[]{:S(2)}, u32[]{:S(2)}) collective-permute-start(bf16[64,116]{1,0:T(8,128)(2,1)S(1)} %get-tuple-element.14), channel_id=1, source_target_pairs={{0,32},{16,48},{32,64},{48,80},{64,96},{80,112},{96,0},{112,16},{1... | collective-permute-start | bytes 44552 | tf_op jit(solution)/shard_map/ppermute | solution.py:45
  70.4 3.8 %collective-permute-start.7 = (bf16[64,116]{1,0:T(8,128)(2,1)S(1)}, bf16[64,116]{1,0:T(8,128)(2,1)S(1)}, u32[]{:S(2)}, u32[]{:S(2)}) collective-permute-start(bf16[64,116]{1,0:T(8,128)(2,1)S(1)} %get-tuple-element.15), channel_id=1, source_target_pairs={{0,96},{16,112},{32,0},{48,16},{64,32},{80,48},{96,64},{112,80},{1... | collective-permute-start | bytes 44552 | tf_op jit(solution)/shard_map/ppermute | solution.py:45
  73.0 4.1 %collective-permute-start.6 = (bf16[64,116]{1,0:T(8,128)(2,1)S(1)}, bf16[64,116]{1,0:T(8,128)(2,1)S(1)}, u32[]{:S(2)}, u32[]{:S(2)}) collective-permute-start(bf16[64,116]{1,0:T(8,128)(2,1)S(1)} %get-tuple-element.16), channel_id=1, source_target_pairs={{0,64},{16,80},{32,96},{48,112},{64,0},{80,16},{96,32},{112,48},{1... | collective-permute-start | bytes 44552 | tf_op jit(solution)/shard_map/ppermute | solution.py:45

commit v3 on v2

--- a/solution.py
+++ b/solution.py
@@ -29,7 +29,6 @@
 RESULT = ROWS + OWN * QKV_BLOCKS
 VM = pl.BlockSpec(memory_space=pltpu.VMEM)
 SM = pl.BlockSpec(memory_space=pltpu.SMEM)
-HB = pl.BlockSpec(memory_space=pl.ANY)
 PARAMS = pltpu.CompilerParams(vmem_limit_bytes=16 << 20)
 
 
@@ -37,6 +36,17 @@
     return pltpu.with_memory_space_constraint(x, pltpu.VMEM)
 
 
+def hold_kernel(mine, out, sem):
+    copy = pltpu.make_async_copy(mine, out, sem)
+    copy.start()
+    copy.wait()
+
+
+def pair_kernel(mine, other, out):
+    out[0] = mine[...]
+    out[1] = other[...]
+
+
 def swap_core(x):
     return lax.ppermute(x, "gx", [(i, i ^ 1) for i in range(8)])
 
@@ -47,11 +57,6 @@
 
 def chunks(total, step):
     return [(at, min(step, total - at)) for at in range(0, total, step)]
-
-
-def place():
-    at = lax.axis_index("gx")
-    return lax.div(at, 2), lax.rem(at, 2)
 
 
 def three(value):
@@ -64,7 +69,8 @@
 
 
 def product_kernel(g0, g1, g2, g3, gm, bm, ga, ba, w_up, w_qkv, out, blocks, flat, spread, side):
-    z, core = place()
+    at = lax.axis_index("gx")
+    z, core = lax.div(at, 2), lax.rem(at, 2)
     narrow = g0.shape[2]
     wide = 8 * narrow
     for k, g in enumerate((g0, g1, g2, g3)):
@@ -182,18 +188,17 @@
             pieces.append(jnp.where(first, pltpu.roll(turned, HD, 1), 0.0))
         query = jnp.concatenate(pieces, axis=0)
         key = query[15:16]
+        query = query * factor
         value = jnp.where(first, 0.0, pltpu.roll(qkv[7:8, LANES:], HD, 1))
-        new_kv[r] = (key + value).astype(BF)
+        new_kv[r : r + 1, :] = (key + value).astype(BF)
         keys = cache[r, 0]
         scores = lax.dot_general(
             query.astype(BF), keys, (((1,), (1,)), ((), ())), preferred_element_type=F32
         )
-        scores = scores * factor
-        live = position < lengths[r]
-        scores = jnp.where(live, scores, -1e30)
-        own = jnp.sum(query * key, axis=1, keepdims=True) * factor
+        scores = jnp.where(position < lengths[r], scores, -jnp.inf)
+        own = jnp.sum(query * key, axis=1, keepdims=True)
         top = jnp.maximum(jnp.max(scores, axis=1, keepdims=True), own)
-        probs = jnp.where(live, jnp.exp(scores - top), 0.0)
+        probs = jnp.exp(scores - top)
         own_prob = jnp.exp(own - top)
         total = jnp.sum(probs, axis=1, keepdims=True) + own_prob
         summed = jnp.dot(probs.astype(BF), keys, preferred_element_type=F32)
@@ -206,10 +211,9 @@
             block[lo : lo + QKV_BLOCKS, h * LANES : (h + 1) * LANES] = pairs.astype(BF)
 
 
-def last_kernel(every, w_down, w_out, keep, send, spread, blocks):
-    z, core = place()
+def last_kernel(every, w_down, w_out, out, spread):
     up_cols, attn_cols = w_down.shape[1], w_out.shape[1]
-    narrow = keep.shape[2]
+    narrow = out.shape[2]
     both = (((1,), (1,)), ((), ()))
     step = OWN * QKV_BLOCKS
     for d in range(GY):
@@ -228,11 +232,7 @@
             left[:, :size], w_out[:, at : at + size], both, preferred_element_type=F32
         )
     for i in range(8):
-        blocks[i] = part[:, narrow * i : narrow * (i + 1)]
-    for k in range(4):
-        at = lax.rem(z + k, 4)
-        keep[k] = blocks[2 * at + core]
-        send[k] = blocks[2 * at + 1 - core]
+        out[i] = part[:, narrow * i : narrow * (i + 1)].astype(BF)
 
 
 def local(
@@ -241,9 +241,27 @@
     rows, narrow = tokens.shape
     wide = gain_attn.shape[0]
 
-    pair = jnp.stack([tokens, swap_core(tokens)])
+    mine = pl.pallas_call(
+        hold_kernel,
+        out_shape=pltpu.VMEM((rows, narrow), BF),
+        in_specs=[pl.BlockSpec(memory_space=pl.ANY)],
+        out_specs=VM,
+        scratch_shapes=[pltpu.SemaphoreType.DMA],
+        compiler_params=pltpu.CompilerParams(vmem_limit_bytes=1 << 20),
+        cost_estimate=pl.CostEstimate(flops=20 << 30, bytes_accessed=96 << 20, transcendentals=0),
+        name="hold",
+    )(pltpu.with_memory_space_constraint(tokens, pltpu.HBM))
+    pair = pl.pallas_call(
+        pair_kernel,
+        out_shape=jax.ShapeDtypeStruct((2, rows, narrow), BF),
+        in_specs=[VM] * 2,
+        out_specs=VM,
+        compiler_params=pltpu.CompilerParams(vmem_limit_bytes=1 << 20),
+        name="pair",
+    )(in_vmem(mine), swap_core(tokens))
     got = [pair] + [shift_z(pair, k) for k in (1, 2, 3)]
     vectors = [v.reshape(1, wide) for v in (gain_mlp, bias_mlp, gain_attn, bias_attn)]
+    held = vectors + [w_up, w_qkv]
     payload = pl.pallas_call(
         product_kernel,
         out_shape=jax.ShapeDtypeStruct((GY, PAYLOAD, BLOCK), BF),
@@ -257,7 +275,7 @@
         ],
         compiler_params=PARAMS,
         name="product",
-    )(*got, *vectors, in_vmem(w_up), in_vmem(w_qkv))
+    )(*got, *[in_vmem(x) for x in held])
 
     steps = np.arange(HD // 2, dtype=np.float64) * (2.0 / HD)
     inverse = jnp.asarray(np.tile(np.power(THETA, -steps), 4)[None].astype(np.float32))
@@ -266,7 +284,7 @@
         functools.partial(middle_kernel, wide),
         out_shape=(
             jax.ShapeDtypeStruct((RESULT, BLOCK), BF),
-            jax.ShapeDtypeStruct((OWN, 1, 2 * HD), BF),
+            jax.ShapeDtypeStruct((OWN, 2 * HD), BF),
         ),
         in_specs=[SM] + [VM] * 3,
         out_specs=(VM, VM),
@@ -276,27 +294,19 @@
     )(lengths, summed, inverse, in_vmem(cache))
 
     every = lax.all_to_all(jnp.broadcast_to(block[None], (GY, RESULT, BLOCK)), "gy", 0, 0)
-    half = jax.ShapeDtypeStruct((4, rows, narrow), F32)
-    keep, send = pl.pallas_call(
+    shares = pl.pallas_call(
         last_kernel,
-        out_shape=(half, half),
+        out_shape=jax.ShapeDtypeStruct((8, rows, narrow), BF),
         in_specs=[VM] * 3,
-        out_specs=(VM, VM),
-        scratch_shapes=[
-            pltpu.VMEM((2, rows * QKV_BLOCKS, LANES), F32),
-            pltpu.VMEM((8, rows, narrow), F32),
-        ],
+        out_specs=VM,
+        scratch_shapes=[pltpu.VMEM((2, rows * QKV_BLOCKS, LANES), F32)],
         compiler_params=PARAMS,
         name="last",
     )(every, in_vmem(w_down.T), in_vmem(w_out.T))
 
-    keep = keep + swap_core(send)
-    narrowed = keep.astype(BF)
-    total = keep[0]
-    for k in (1, 2, 3):
-        total = total + shift_z(narrowed[k], k).astype(F32)
-    mixed = (tokens.astype(F32) + total).astype(BF)
-    return (mixed, new_kv)
+    merged = jnp.sum(lax.all_to_all(shares, "gx", 0, 0).astype(F32), axis=0)
+    mixed = (tokens.astype(F32) + merged).astype(BF)
+    return (mixed, new_kv.reshape(OWN, 1, 2 * HD))
 
 
 def solution(mesh):

time: 78.8 us -> 70 us (0.89); the launches traced: 77.7 us -> 69.7 us
  blocking collectives: 34.5 us -> 47.2 us
  local copies, waits for them, and re-layouts: 8.45 us -> 0.13 us
  starting transfers between devices: 13.6 us -> 6.22 us
  waiting for transfers between devices: 9.19 us -> 3.8 us
  Pallas kernels: 9.92 us -> 10.9 us
    all_to_all x0 -> x1, blocking collectives: none -> 12.3 us  [local(): merged = jnp.sum(lax.all_to_all(shares, 'gx', 0, 0).astype(F32), axis=0)]
    unnamed x25 -> x26, local copies, waits for them, and re-layouts: 8.37 us -> 0.07 us
    ppermute x2 -> x1, starting transfers between devices: 6.24 us -> 1.5 us  [swap_core(): return lax.ppermute(x, 'gx', [(i, i ^ 1) for i in range(8)])]
    ppermute x6 -> x3, waiting for transfers between devices: 7.15 us -> 3.63 us  [shift_z(): return lax.ppermute(x, 'gx', [(i, (i + 2 * k) % 8) for i in range(8)])]
    ppermute x6 -> x3, starting transfers between devices: 7.35 us -> 4.72 us  [shift_z(): return lax.ppermute(x, 'gx', [(i, (i + 2 * k) % 8) for i in range(8)])]
    ppermute x2 -> x1, waiting for transfers between devices: 2.04 us -> 0.16 us  [swap_core(): return lax.ppermute(x, 'gx', [(i, i ^ 1) for i in range(8)])]
    pallas_call x1 -> x3, Pallas kernels: 3.23 us -> 4.05 us  [the longest x1 3.17 us: local(): pl.pallas_call(last_kernel, out_shape=jax.ShapeDtypeStruct((8, rows, narr...]
  transfers between devices with their start and end apart: 8 -> 4, of which waited for: 6 -> 3; matrix products, arithmetic and copies ran while one was open for 1% -> 0% of each run, Pallas kernels for 0% -> 1%
where the time goes in v3:
time: 70 us; the launch traced here: 69.7 us
  blocking collectives  47.2 us (67%)
  Pallas kernels  10.9 us (16%)
  starting transfers between devices  6.22 us (9%)
  waiting for transfers between devices  3.8 us (5%)
  between operations  0.83 us (1%)
    all_to_all x1, blocking collectives, local(): summed = lax.all_to_all(payload, 'gy', 0, 0)  21.1 us
    all_to_all x1, blocking collectives, local(): lax.all_to_all(jnp.broadcast_to(block[None], (GY, RESULT, BLOCK)), 'gy',...  13.7 us
    all_to_all x1, blocking collectives, local(): merged = jnp.sum(lax.all_to_all(shares, 'gx', 0, 0).astype(F32), axis=0)  12.3 us
    ppermute x3, starting transfers between devices, shift_z(): return lax.ppermute(x, 'gx', [(i, (i + 2 * k) % 8) for i in range(8)])  4.72 us
    pallas_call x1, Pallas kernels, local(): pl.pallas_call(functools.partial(middle_kernel, wide), out_shape=(jax.Sha...  4.66 us
    ppermute x3, waiting for transfers between devices, shift_z(): return lax.ppermute(x, 'gx', [(i, (i + 2 * k) % 8) for i in range(8)])  3.63 us
    pallas_call x1, Pallas kernels, local(): pl.pallas_call(last_kernel, out_shape=jax.ShapeDtypeStruct((8, rows, narr...  3.17 us
    pallas_call x1, Pallas kernels, local(): pl.pallas_call(product_kernel, out_shape=jax.ShapeDtypeStruct((GY, PAYLOA...  2.23 us
  transfers between devices with their start and end apart: 4, of which 3 were waited for; matrix products, arithmetic and copies ran while one was open for 0% of the time, Pallas kernels for 1%

profile of v3, /device:TPU:1, one launch (start us, length us, event | category | flops | bytes accessed | tf_op | source)
XLA Modules:
  0.0 69.7 jit_solution(13065166477526525962)
XLA Ops:
  0.6 0.0 copy-start.2
  0.6 0.0 copy-start.5
  0.7 0.0 copy-start.4
  0.7 0.0 copy-start.7
  0.7 0.0 copy-start.6
  0.7 1.5 %collective-permute-start = (bf16[64,116]{1,0:T(8,128)(2,1)}, bf16[64,116]{1,0:T(8,128)(2,1)S(1)}, u32[]{:S(2)}, u32[]{:S(2)}) collective-permute-start(bf16[64,116]{1,0:T(8,128)(2,1)} %mine.1), channel_id=1, source_target_pairs={{0,16},{16,0},{32,48},{48,32},{64,80},{80,64},{96,112},{112,96},{1... | collective-permute-start | bytes 44552 | tf_op jit(solution)/shard_map/ppermute | solution.py:51
  2.2 0.0 copy-start
  2.2 0.9 %hold.1.mine = bf16[64,116]{1,0:T(8,128)(2,1)S(1)} custom-call(bf16[64,116]{1,0:T(8,128)(2,1)} %mine.1), custom_call_target="tpu_custom_call" | custom-call | flops 21474836480 | bytes 100663296 | tf_op jit(solution)/shard_map/hold/pallas_call | solution.py:244
  3.1 0.2 collective-permute-done.other
  3.2 4.0 %collective-permute-start.3 = (bf16[2,64,116]{2,1,0:T(8,128)(2,1)S(1)}, bf16[2,64,116]{2,1,0:T(8,128)(2,1)S(1)}, u32[]{:S(2)}, u32[]{:S(2)}) collective-permute-start(bf16[2,64,116]{2,1,0:T(8,128)(2,1)S(1)} %pair.1.g0), channel_id=1, source_target_pairs={{0,96},{16,112},{32,0},{48,16},{64,32},{80,48},{96,64},{112,80},{1... | collective-permute-start | bytes 89096 | tf_op jit(solution)/shard_map/ppermute | solution.py:55
  7.3 0.0 collective-permute-start.2
  7.3 0.7 %collective-permute-start.1 = (bf16[2,64,116]{2,1,0:T(8,128)(2,1)S(1)}, bf16[2,64,116]{2,1,0:T(8,128)(2,1)S(1)}, u32[]{:S(2)}, u32[]{:S(2)}) collective-permute-start(bf16[2,64,116]{2,1,0:T(8,128)(2,1)S(1)} %pair.1.g0), channel_id=1, source_target_pairs={{0,32},{16,48},{32,64},{48,80},{64,96},{80,112},{96,0},{112,16},{1... | collective-permute-start | bytes 89096 | tf_op jit(solution)/shard_map/ppermute | solution.py:55
  8.0 0.3 collective-permute-done.3.g3
  8.3 3.3 %collective-permute-done.2.g2 = bf16[2,64,116]{2,1,0:T(8,128)(2,1)S(1)} collective-permute-done((bf16[2,64,116]{2,1,0:T(8,128)(2,1)S(1)}, bf16[2,64,116]{2,1,0:T(8,128)(2,1)S(1)}, u32[]{:S(2)}, u32[]{:S(2)}) %collective-permute-start.2) | collective-permute-done | bytes 29728 | tf_op jit(solution)/shard_map/ppermute | solution.py:55
  11.6 0.0 collective-permute-done.1.g1
  11.6 0.0 slice-start
  11.6 0.0 copy-done.2
  11.6 0.0 copy-done.5
  11.6 0.0 copy-done.4
  11.6 0.0 copy-done.7
  11.6 0.0 copy-done.6
  11.6 0.0 copy-done
  11.6 0.0 copy-start.1
  11.7 0.0 copy-start.8
  11.7 0.0 copy-start.9
  11.7 0.0 slice-start.1
  11.7 2.2 %product.1 = bf16[16,120,256]{2,1,0:T(8,128)(2,1)S(1)} custom-call(bf16[2,64,116]{2,1,0:T(8,128)(2,1)S(1)} %pair.1.g0, bf16[2,64,116]{2,1,0:T(8,128)(2,1)S(1)} %collective-permute-done.1.g1, bf16[2,64,116]{2,1,0:T(8,128)(2,1)S(1)} %collective-permute-done.2.g2, bf16[2,64,116]{2,1,0:T(8,128)(2,1)S(1)} %collective-permute-done.3.g3, f32[1,928]{1,0:T(1,128)S(1)} %bitcast.11, ...), custom_call_target="tpu_custom_call" | custom-call | tf_op jit(solution)/shard_map/product/pallas_call | solution.py:265
  13.9 21.1 %all_to_all.15.got = bf16[16,120,256]{2,1,0:T(8,128)(2,1)S(1)} all-to-all(bf16[16,120,256]{2,1,0:T(8,128)(2,1)S(1)} %product.1), channel_id=1, replica_groups=mesh['gx'=8,'gy'=16] {'gy'}, dimensions={0} | all-to-all | bytes 1966080 | tf_op jit(solution)/shard_map/all_to_all | solution.py:282
  35.1 0.0 copy-done.1
  35.1 0.0 copy-done.8
  35.1 0.0 copy-done.9
  35.1 0.0 copy-start.3
  35.1 4.7 %middle.1 = (bf16[96,256]{1,0:T(8,128)(2,1)S(1)}, bf16[4,128]{1,0:T(4,128)(2,1)}) custom-call(s32[4]{0:T(128)S(1)} %copy-done.8, bf16[16,120,256]{2,1,0:T(8,128)(2,1)S(1)} %all_to_all.15.got, f32[1,128]{1,0:T(1,128)S(1)} %copy-done.9, bf16[4,1,4096,128]{3,2,1,0:T(8,128)(2,1)S(1)} %copy-done.1), custom_call_target="tpu_custom_call" | custom-call | tf_op jit(solution)/shard_map/middle/pallas_call | solution.py:283
  39.8 0.1 broadcast_in_dim.2
  39.8 13.7 %all_to_all.16.every = bf16[16,96,256]{2,1,0:T(8,128)(2,1)S(1)} all-to-all(bf16[16,96,256]{2,1,0:T(8,128)(2,1)S(1)} %broadcast_in_dim.2), channel_id=1, replica_groups=mesh['gx'=8,'gy'=16] {'gy'}, dimensions={0} | all-to-all | bytes 1572864 | tf_op jit(solution)/shard_map/all_to_all | solution.py:296
  53.6 0.0 slice-done
  53.6 0.0 slice-done.1
  53.6 0.0 copy-done.3
  53.6 0.0 copy-start.10
  53.6 3.2 %last.1 = bf16[8,64,116]{2,1,0:T(8,128)(2,1)S(1)} custom-call(bf16[16,96,256]{2,1,0:T(8,128)(2,1)S(1)} %all_to_all.16.every, bf16[928,3712]{1,0:T(8,128)(2,1)S(1)} %bitcast.9, bf16[928,1856]{1,0:T(8,128)(2,1)S(1)} %bitcast.10), custom_call_target="tpu_custom_call" | custom-call | tf_op jit(solution)/shard_map/last/pallas_call | solution.py:297
  56.8 12.3 %all_to_all.17 = bf16[8,64,116]{2,1,0:T(8,128)(2,1)S(1)} all-to-all(bf16[8,64,116]{2,1,0:T(8,128)(2,1)S(1)} %last.1), channel_id=1, replica_groups=mesh['gx'=8,'gy'=16] {'gx'}, dimensions={0} | all-to-all | bytes 237568 | tf_op jit(solution)/shard_map/all_to_all | solution.py:307
  69.1 0.0 copy-done.10
  69.1 0.6 add_convert_fusion
  (3 shorter events, 0.0 us)
Async XLA Ops:
  0.6 11.0 %copy-start.2 = (bf16[928,1984]{1,0:T(8,128)(2,1)S(1)}, bf16[928,1984]{1,0:T(8,128)(2,1)}, u32[]{:S(2)}) copy-start(bf16[928,1984]{1,0:T(8,128)(2,1)} %w_qkv.1) | copy-start | bytes 11046916
  0.6 11.0 %copy-start.5 = (f32[928]{0:T(1024)S(1)}, f32[928]{0:T(1024)}, u32[]{:S(2)}) copy-start(f32[928]{0:T(1024)} %param.17) | copy-start | bytes 11140
  0.7 11.0 %copy-start.4 = (f32[928]{0:T(1024)S(1)}, f32[928]{0:T(1024)}, u32[]{:S(2)}) copy-start(f32[928]{0:T(1024)} %param.16) | copy-start | bytes 11140
  0.7 11.0 %copy-start.7 = (f32[928]{0:T(1024)S(1)}, f32[928]{0:T(1024)}, u32[]{:S(2)}) copy-start(f32[928]{0:T(1024)} %param.15) | copy-start | bytes 11140
  0.7 11.0 %copy-start.6 = (f32[928]{0:T(1024)S(1)}, f32[928]{0:T(1024)}, u32[]{:S(2)}) copy-start(f32[928]{0:T(1024)} %param.14) | copy-start | bytes 11140
  0.7 2.6 %collective-permute-start = (bf16[64,116]{1,0:T(8,128)(2,1)}, bf16[64,116]{1,0:T(8,128)(2,1)S(1)}, u32[]{:S(2)}, u32[]{:S(2)}) collective-permute-start(bf16[64,116]{1,0:T(8,128)(2,1)} %mine.1), channel_id=1, source_target_pairs={{0,16},{16,0},{32,48},{48,32},{64,80},{80,64},{96,112},{112,96},{1... | collective-permute-start | bytes 44552 | tf_op jit(solution)/shard_map/ppermute | solution.py:51
  2.2 9.5 %copy-start = (bf16[928,3712]{1,0:T(8,128)(2,1)S(1)}, bf16[928,3712]{1,0:T(8,128)(2,1)}, u32[]{:S(2)}) copy-start(bf16[928,3712]{1,0:T(8,128)(2,1)} %w_up.1) | copy-start | bytes 20668420
  3.2 5.0 %collective-permute-start.3 = (bf16[2,64,116]{2,1,0:T(8,128)(2,1)S(1)}, bf16[2,64,116]{2,1,0:T(8,128)(2,1)S(1)}, u32[]{:S(2)}, u32[]{:S(2)}) collective-permute-start(bf16[2,64,116]{2,1,0:T(8,128)(2,1)S(1)} %pair.1.g0), channel_id=1, source_target_pairs={{0,96},{16,112},{32,0},{48,16},{64,32},{80,48},{96,64},{112,80},{1... | collective-permute-start | bytes 89096 | tf_op jit(solution)/shard_map/ppermute | solution.py:55
  7.3 4.3 %collective-permute-start.2 = (bf16[2,64,116]{2,1,0:T(8,128)(2,1)S(1)}, bf16[2,64,116]{2,1,0:T(8,128)(2,1)S(1)}, u32[]{:S(2)}, u32[]{:S(2)}) collective-permute-start(bf16[2,64,116]{2,1,0:T(8,128)(2,1)S(1)} %pair.1.g0), channel_id=1, source_target_pairs={{0,64},{16,80},{32,96},{48,112},{64,0},{80,16},{96,32},{112,48},{1... | collective-permute-start | bytes 89096 | tf_op jit(solution)/shard_map/ppermute | solution.py:55
  7.3 4.3 %collective-permute-start.1 = (bf16[2,64,116]{2,1,0:T(8,128)(2,1)S(1)}, bf16[2,64,116]{2,1,0:T(8,128)(2,1)S(1)}, u32[]{:S(2)}, u32[]{:S(2)}) collective-permute-start(bf16[2,64,116]{2,1,0:T(8,128)(2,1)S(1)} %pair.1.g0), channel_id=1, source_target_pairs={{0,32},{16,48},{32,64},{48,80},{64,96},{80,112},{96,0},{112,16},{1... | collective-permute-start | bytes 89096 | tf_op jit(solution)/shard_map/ppermute | solution.py:55
  11.6 42.0 %slice-start = ((s8[6889472]{0:T(1024)(128)(4,1)}), s8[4194304]{0:T(1024)(128)(4,1)S(1)}, s32[]{:S(2)}) async-start(s8[6889472]{0:T(1024)(128)(4,1)} %bitcast.7), calls=%async_computation.3 | async-start | bytes 8388608
  11.6 23.4 %copy-start.1 = (bf16[4,1,4096,128]{3,2,1,0:T(8,128)(2,1)S(1)}, bf16[4,1,4096,128]{3,2,1,0:T(8,128)(2,1)}, u32[]{:S(2)}) copy-start(bf16[4,1,4096,128]{3,2,1,0:T(8,128)(2,1)} %cache.1) | copy-start | bytes 12582916
  11.7 23.4 %copy-start.8 = (s32[4]{0:T(128)S(1)}, s32[4]{0:T(128)}, u32[]{:S(2)}) copy-start(s32[4]{0:T(128)} %lengths.1) | copy-start | bytes 52
  11.7 23.4 %copy-start.9 = (f32[1,128]{1,0:T(1,128)S(1)}, f32[1,128]{1,0:T(1,128)}, u32[]{:S(2)}) copy-start(f32[1,128]{1,0:T(1,128)} %constant.4.clone.inverse) | copy-start | bytes 1540
  11.7 41.9 %slice-start.1 = ((s8[6889472]{0:T(1024)(128)(4,1)}), s8[2695168]{0:T(1024)(128)(4,1)S(1)}, s32[]{:S(2)}) async-start(s8[6889472]{0:T(1024)(128)(4,1)} %bitcast.7), calls=%async_computation.4 | async-start | bytes 5390336
  35.1 18.5 %copy-start.3 = (bf16[1856,928]{0,1:T(8,128)(2,1)S(1)}, bf16[1856,928]{0,1:T(8,128)(2,1)}, u32[]{:S(2)}) copy-start(bf16[1856,928]{0,1:T(8,128)(2,1)} %param.19) | copy-start | bytes 10334212
  53.6 15.5 %copy-start.10 = (bf16[64,116]{1,0:T(8,128)(2,1)S(1)}, bf16[64,116]{1,0:T(8,128)(2,1)}, u32[]{:S(2)}) copy-start(bf16[64,116]{1,0:T(8,128)(2,1)} %mine.1) | copy-start | bytes 44548

commit v4 on v3

--- a/solution.py
+++ b/solution.py
@@ -146,16 +146,6 @@
     columns[...] = jnp.transpose(table)
     whole = columns[:ROWS]
 
-    acc = jnp.zeros((ROWS, BLOCK), F32)
-    plain = jnp.zeros((1, BLOCK), F32)
-    for d in range(GY):
-        side = got[d, AT_SIDE:AT_QKV, :].astype(F32)
-        acc = acc + (got[d, :ROWS, :].astype(F32) + whole[:, d : d + 1] * side[0:1])
-        plain = plain + side[1:2]
-    up = whole[:, GY : GY + 1] * acc + plain
-    hidden = 0.5 * up * (1.0 + lax.erf(up * math.sqrt(0.5)))
-    block[:ROWS, :] = hidden.astype(BF)
-
     plain = jnp.zeros((QKV_BLOCKS, BLOCK), F32)
     for d in range(GY):
         plain = plain + got[d, AT_BIAS:, :].astype(F32)
@@ -165,6 +155,8 @@
     length = cache.shape[2]
     position = lax.broadcasted_iota(jnp.int32, (1, length), 1)
     factor = 1.0 / math.sqrt(HD)
+
+    queries, keys_new, values_new = [], [], []
     for r in range(OWN):
         mine = columns[pl.ds(own_at + r, 1), :]
         acc = jnp.zeros((QKV_BLOCKS, BLOCK), F32)
@@ -188,21 +180,29 @@
             pieces.append(jnp.where(first, pltpu.roll(turned, HD, 1), 0.0))
         query = jnp.concatenate(pieces, axis=0)
         key = query[15:16]
-        query = query * factor
         value = jnp.where(first, 0.0, pltpu.roll(qkv[7:8, LANES:], HD, 1))
         new_kv[r : r + 1, :] = (key + value).astype(BF)
-        keys = cache[r, 0]
+        queries.append(query * factor)
+        keys_new.append(key)
+        values_new.append(value)
+
+    def score(r):
         scores = lax.dot_general(
-            query.astype(BF), keys, (((1,), (1,)), ((), ())), preferred_element_type=F32
+            queries[r].astype(BF), cache[r, 0], (((1,), (1,)), ((), ())), preferred_element_type=F32
         )
-        scores = jnp.where(position < lengths[r], scores, -jnp.inf)
-        own = jnp.sum(query * key, axis=1, keepdims=True)
+        return jnp.where(position < lengths[r], scores, -jnp.inf)
+
+    def soften(r, scores):
+        own = jnp.sum(queries[r] * keys_new[r], axis=1, keepdims=True)
         top = jnp.maximum(jnp.max(scores, axis=1, keepdims=True), own)
         probs = jnp.exp(scores - top)
         own_prob = jnp.exp(own - top)
         total = jnp.sum(probs, axis=1, keepdims=True) + own_prob
-        summed = jnp.dot(probs.astype(BF), keys, preferred_element_type=F32)
-        summed = summed + own_prob.astype(BF).astype(F32) * value
+        return probs.astype(BF), own_prob, total
+
+    def mix(r, probs, own_prob, total):
+        summed = jnp.dot(probs, cache[r, 0], preferred_element_type=F32)
+        summed = summed + own_prob.astype(BF).astype(F32) * values_new[r]
         result = summed / total
         lo = ROWS + QKV_BLOCKS * r
         for h in range(2):
@@ -210,29 +210,65 @@
             pairs = jnp.where(first, pltpu.roll(even, HD, 1), odd)
             block[lo : lo + QKV_BLOCKS, h * LANES : (h + 1) * LANES] = pairs.astype(BF)
 
-
-def last_kernel(every, w_down, w_out, out, spread):
+    soft = {}
+    scores = score(0)
+    for r in range(OWN):
+        following = score(r + 1) if r + 1 < OWN else None
+        soft[r] = soften(r, scores)
+        if r > 0:
+            mix(r - 1, *soft.pop(r - 1))
+        scores = following
+
+    acc = jnp.zeros((ROWS, BLOCK), F32)
+    plain = jnp.zeros((1, BLOCK), F32)
+    for d in range(GY):
+        side = got[d, AT_SIDE:AT_QKV, :].astype(F32)
+        acc = acc + (got[d, :ROWS, :].astype(F32) + whole[:, d : d + 1] * side[0:1])
+        plain = plain + side[1:2]
+    up = whole[:, GY : GY + 1] * acc + plain
+    hidden = 0.5 * up * (1.0 + lax.erf(up * math.sqrt(0.5)))
+    block[:ROWS, :] = hidden.astype(BF)
+    mix(OWN - 1, *soft.pop(OWN - 1))
+
+
+def last_kernel(every, w_down, w_out, out, spread, left, turned):
     up_cols, attn_cols = w_down.shape[1], w_out.shape[1]
-    narrow = out.shape[2]
-    both = (((1,), (1,)), ((), ()))
+    narrow = w_down.shape[0] // 8
     step = OWN * QKV_BLOCKS
     for d in range(GY):
         for h in range(2):
             cols = slice(h * LANES, (h + 1) * LANES)
             spread[h, d * step : (d + 1) * step, :] = every[d, ROWS:, cols].astype(F32)
-    part = jnp.zeros((ROWS, w_down.shape[0]), F32)
     for d, (at, size) in enumerate(chunks(up_cols, BLOCK)):
-        part = part + lax.dot_general(
-            every[d, :ROWS, :size], w_down[:, at : at + size], both, preferred_element_type=F32
-        )
-    for b, (at, size) in enumerate(chunks(attn_cols, BLOCK)):
-        left = [spread[h, pl.ds(b, ROWS, stride=QKV_BLOCKS), :].astype(BF) for h in range(2)]
-        left = jnp.concatenate(left, axis=1)
-        part = part + lax.dot_general(
-            left[:, :size], w_out[:, at : at + size], both, preferred_element_type=F32
-        )
+        part = every[d, :ROWS, :size]
+        left[:ROWS, at : at + size] = part
+        left[ROWS:, at : at + size] = part
+    for t in range(-(-attn_cols // LANES)):
+        part = spread[t % 2, pl.ds(t // 2, ROWS, stride=QKV_BLOCKS), :].astype(BF)
+        at = up_cols + t * LANES
+        left[:ROWS, at : at + LANES] = part
+        left[ROWS:, at : at + LANES] = part
+    both = (((1,), (1,)), ((), ()))
+    total = lax.dot_general(w_down[...], left[:, :up_cols], both, preferred_element_type=F32)
+    total = total + lax.dot_general(
+        w_out[...], left[:, up_cols : up_cols + attn_cols], both, preferred_element_type=F32
+    )
+    turned[: 8 * narrow, :] = total
+    turned[8 * narrow :, :] = jnp.zeros((turned.shape[0] - 8 * narrow, LANES), F32)
+    first = lax.broadcasted_iota(jnp.int32, (1, LANES), 1) < ROWS
     for i in range(8):
-        out[i] = part[:, narrow * i : narrow * (i + 1)].astype(BF)
+        at = narrow * i
+        upper, lower = turned[at : at + ROWS, :], turned[at + ROWS : at + 2 * ROWS, :]
+        out[i] = jnp.where(first, upper, lower).astype(BF)
+
+
+def finish_kernel(shares, tokens, mixed):
+    total = shares[0].astype(F32)
+    for i in range(1, 8):
+        total = total + shares[i].astype(F32)
+    total = jnp.transpose(total)
+    total = jnp.concatenate([total[:ROWS], total[ROWS:]], axis=1)[:, : tokens.shape[1]]
+    mixed[...] = (tokens[...].astype(F32) + total).astype(BF)
 
 
 def local(
@@ -296,16 +332,26 @@
     every = lax.all_to_all(jnp.broadcast_to(block[None], (GY, RESULT, BLOCK)), "gy", 0, 0)
     shares = pl.pallas_call(
         last_kernel,
-        out_shape=jax.ShapeDtypeStruct((8, rows, narrow), BF),
+        out_shape=jax.ShapeDtypeStruct((8, ROWS, LANES), BF),
         in_specs=[VM] * 3,
         out_specs=VM,
-        scratch_shapes=[pltpu.VMEM((2, rows * QKV_BLOCKS, LANES), F32)],
+        scratch_shapes=[
+            pltpu.VMEM((2, rows * QKV_BLOCKS, LANES), F32),
+            pltpu.VMEM((2 * rows, w_down.shape[0] + 15 * LANES), BF),
+            pltpu.VMEM((8 * narrow + 16, LANES), F32),
+        ],
         compiler_params=PARAMS,
         name="last",
     )(every, in_vmem(w_down.T), in_vmem(w_out.T))
 
-    merged = jnp.sum(lax.all_to_all(shares, "gx", 0, 0).astype(F32), axis=0)
-    mixed = (tokens.astype(F32) + merged).astype(BF)
+    mixed = pl.pallas_call(
+        finish_kernel,
+        out_shape=jax.ShapeDtypeStruct((rows, narrow), BF),
+        in_specs=[VM] * 2,
+        out_specs=VM,
+        compiler_params=pltpu.CompilerParams(vmem_limit_bytes=1 << 20),
+        name="finish",
+    )(lax.all_to_all(shares, "gx", 0, 0), tokens)
     return (mixed, new_kv.reshape(OWN, 1, 2 * HD))
 
 

time: 70 us -> 68.7 us (0.981)
    pallas_call x1, Pallas kernels: 4.66 us -> 3.44 us  [local(): pl.pallas_call(functools.partial(middle_kernel, wide), out_shape=(jax.Sha...]
    pallas_call x1 -> x2, Pallas kernels: 3.17 us -> 3.79 us  [the longest x1 3.01 us: local(): pl.pallas_call(last_kernel, out_shape=jax.ShapeDtypeStruct((8, ROWS, LANE...]
where the time goes in v4:
time: 68.7 us; the launch traced here: 68.5 us
  blocking collectives  47.2 us (69%)
  Pallas kernels  10.3 us (15%)
  starting transfers between devices  6.22 us (9%)
  waiting for transfers between devices  3.8 us (6%)
  between operations  0.81 us (1%)
    all_to_all x1, blocking collectives, local(): summed = lax.all_to_all(payload, 'gy', 0, 0)  21.1 us
    all_to_all x1, blocking collectives, local(): lax.all_to_all(jnp.broadcast_to(block[None], (GY, RESULT, BLOCK)), 'gy',...  13.7 us
    all_to_all x1, blocking collectives, local(): lax.all_to_all(shares, 'gx', 0, 0)  12.3 us
    ppermute x3, starting transfers between devices, shift_z(): return lax.ppermute(x, 'gx', [(i, (i + 2 * k) % 8) for i in range(8)])  4.72 us
    ppermute x3, waiting for transfers between devices, shift_z(): return lax.ppermute(x, 'gx', [(i, (i + 2 * k) % 8) for i in range(8)])  3.63 us
    pallas_call x1, Pallas kernels, local(): pl.pallas_call(functools.partial(middle_kernel, wide), out_shape=(jax.Sha...  3.44 us
    pallas_call x1, Pallas kernels, local(): pl.pallas_call(last_kernel, out_shape=jax.ShapeDtypeStruct((8, ROWS, LANE...  3.01 us
    pallas_call x1, Pallas kernels, local(): pl.pallas_call(product_kernel, out_shape=jax.ShapeDtypeStruct((GY, PAYLOA...  2.23 us
  transfers between devices with their start and end apart: 4, of which 3 were waited for; matrix products, arithmetic and copies ran while one was open for 0% of the time, Pallas kernels for 1%

profile of v4, /device:TPU:1, one launch (start us, length us, event | category | flops | bytes accessed | tf_op | source)
XLA Modules:
  0.0 68.5 jit_solution(8548189075180079710)
XLA Ops:
  0.6 0.0 copy-start.2
  0.6 0.0 copy-start.6
  0.7 0.0 copy-start.5
  0.7 0.0 copy-start.8
  0.7 0.0 copy-start.7
  0.7 1.5 %collective-permute-start = (bf16[64,116]{1,0:T(8,128)(2,1)}, bf16[64,116]{1,0:T(8,128)(2,1)S(1)}, u32[]{:S(2)}, u32[]{:S(2)}) collective-permute-start(bf16[64,116]{1,0:T(8,128)(2,1)} %tokens.1), channel_id=1, source_target_pairs={{0,16},{16,0},{32,48},{48,32},{64,80},{80,64},{96,112},{112,96},{1... | collective-permute-start | bytes 44552 | tf_op jit(solution)/shard_map/ppermute | solution.py:51
  2.2 0.0 copy-start
  2.2 0.9 %hold.1.mine = bf16[64,116]{1,0:T(8,128)(2,1)S(1)} custom-call(bf16[64,116]{1,0:T(8,128)(2,1)} %tokens.1), custom_call_target="tpu_custom_call" | custom-call | flops 21474836480 | bytes 100663296 | tf_op jit(solution)/shard_map/hold/pallas_call | solution.py:280
  3.1 0.2 collective-permute-done.other
  3.2 4.0 %collective-permute-start.3 = (bf16[2,64,116]{2,1,0:T(8,128)(2,1)S(1)}, bf16[2,64,116]{2,1,0:T(8,128)(2,1)S(1)}, u32[]{:S(2)}, u32[]{:S(2)}) collective-permute-start(bf16[2,64,116]{2,1,0:T(8,128)(2,1)S(1)} %pair.1.g0), channel_id=1, source_target_pairs={{0,96},{16,112},{32,0},{48,16},{64,32},{80,48},{96,64},{112,80},{1... | collective-permute-start | bytes 89096 | tf_op jit(solution)/shard_map/ppermute | solution.py:55
  7.3 0.0 collective-permute-start.2
  7.3 0.7 %collective-permute-start.1 = (bf16[2,64,116]{2,1,0:T(8,128)(2,1)S(1)}, bf16[2,64,116]{2,1,0:T(8,128)(2,1)S(1)}, u32[]{:S(2)}, u32[]{:S(2)}) collective-permute-start(bf16[2,64,116]{2,1,0:T(8,128)(2,1)S(1)} %pair.1.g0), channel_id=1, source_target_pairs={{0,32},{16,48},{32,64},{48,80},{64,96},{80,112},{96,0},{112,16},{1... | collective-permute-start | bytes 89096 | tf_op jit(solution)/shard_map/ppermute | solution.py:55
  8.0 0.3 collective-permute-done.3.g3
  8.3 3.3 %collective-permute-done.2.g2 = bf16[2,64,116]{2,1,0:T(8,128)(2,1)S(1)} collective-permute-done((bf16[2,64,116]{2,1,0:T(8,128)(2,1)S(1)}, bf16[2,64,116]{2,1,0:T(8,128)(2,1)S(1)}, u32[]{:S(2)}, u32[]{:S(2)}) %collective-permute-start.2) | collective-permute-done | bytes 29728 | tf_op jit(solution)/shard_map/ppermute | solution.py:55
  11.6 0.0 collective-permute-done.1.g1
  11.6 0.0 slice-start
  11.6 0.0 copy-done.2
  11.6 0.0 copy-done.6
  11.6 0.0 copy-done.5
  11.6 0.0 copy-done.8
  11.6 0.0 copy-done.7
  11.6 0.0 copy-done
  11.6 0.0 copy-start.1
  11.7 0.0 copy-start.9
  11.7 0.0 copy-start.10
  11.7 0.0 slice-start.1
  11.7 2.2 %product.1 = bf16[16,120,256]{2,1,0:T(8,128)(2,1)S(1)} custom-call(bf16[2,64,116]{2,1,0:T(8,128)(2,1)S(1)} %pair.1.g0, bf16[2,64,116]{2,1,0:T(8,128)(2,1)S(1)} %collective-permute-done.1.g1, bf16[2,64,116]{2,1,0:T(8,128)(2,1)S(1)} %collective-permute-done.2.g2, bf16[2,64,116]{2,1,0:T(8,128)(2,1)S(1)} %collective-permute-done.3.g3, f32[1,928]{1,0:T(1,128)S(1)} %bitcast.11, ...), custom_call_target="tpu_custom_call" | custom-call | tf_op jit(solution)/shard_map/product/pallas_call | solution.py:301
  13.9 21.1 %all_to_all.15.got = bf16[16,120,256]{2,1,0:T(8,128)(2,1)S(1)} all-to-all(bf16[16,120,256]{2,1,0:T(8,128)(2,1)S(1)} %product.1), channel_id=1, replica_groups=mesh['gx'=8,'gy'=16] {'gy'}, dimensions={0} | all-to-all | bytes 1966080 | tf_op jit(solution)/shard_map/all_to_all | solution.py:318
  35.1 0.0 copy-done.1
  35.1 0.0 copy-done.9
  35.1 0.0 copy-done.10
  35.1 0.0 copy-start.3
  35.1 3.4 %middle.1 = (bf16[96,256]{1,0:T(8,128)(2,1)S(1)}, bf16[4,128]{1,0:T(4,128)(2,1)}) custom-call(s32[4]{0:T(128)S(1)} %copy-done.9, bf16[16,120,256]{2,1,0:T(8,128)(2,1)S(1)} %all_to_all.15.got, f32[1,128]{1,0:T(1,128)S(1)} %copy-done.10, bf16[4,1,4096,128]{3,2,1,0:T(8,128)(2,1)S(1)} %copy-done.1), custom_call_target="tpu_custom_call" | custom-call | tf_op jit(solution)/shard_map/middle/pallas_call | solution.py:319
  38.5 0.1 broadcast_in_dim.2
  38.6 13.7 %all_to_all.16.every = bf16[16,96,256]{2,1,0:T(8,128)(2,1)S(1)} all-to-all(bf16[16,96,256]{2,1,0:T(8,128)(2,1)S(1)} %broadcast_in_dim.2), channel_id=1, replica_groups=mesh['gx'=8,'gy'=16] {'gy'}, dimensions={0} | all-to-all | bytes 1572864 | tf_op jit(solution)/shard_map/all_to_all | solution.py:332
  52.4 0.0 slice-done
  52.4 0.0 slice-done.1
  52.4 0.0 copy-done.3
  52.4 0.0 copy-start.4
  52.4 3.0 %last.1 = bf16[8,64,128]{2,1,0:T(8,128)(2,1)S(1)} custom-call(bf16[16,96,256]{2,1,0:T(8,128)(2,1)S(1)} %all_to_all.16.every, bf16[928,3712]{1,0:T(8,128)(2,1)S(1)} %bitcast.9, bf16[928,1856]{1,0:T(8,128)(2,1)S(1)} %bitcast.10), custom_call_target="tpu_custom_call" | custom-call | tf_op jit(solution)/shard_map/last/pallas_call | solution.py:333
  55.4 12.3 %all_to_all.17.shares = bf16[8,64,128]{2,1,0:T(8,128)(2,1)S(1)} all-to-all(bf16[8,64,128]{2,1,0:T(8,128)(2,1)S(1)} %last.1), channel_id=1, replica_groups=mesh['gx'=8,'gy'=16] {'gx'}, dimensions={0} | all-to-all | bytes 262144 | tf_op jit(solution)/shard_map/all_to_all | solution.py:354
  67.7 0.0 copy-done.4
  67.7 0.8 %finish.1 = bf16[64,116]{1,0:T(8,128)(2,1)} custom-call(bf16[8,64,128]{2,1,0:T(8,128)(2,1)S(1)} %all_to_all.17.shares, bf16[64,116]{1,0:T(8,128)(2,1)S(1)} %copy-done.4), custom_call_target="tpu_custom_call" | custom-call | tf_op jit(solution)/shard_map/finish/pallas_call | solution.py:347
  (2 shorter events, 0.0 us)
Async XLA Ops:
  0.6 11.0 %copy-start.2 = (bf16[928,1984]{1,0:T(8,128)(2,1)S(1)}, bf16[928,1984]{1,0:T(8,128)(2,1)}, u32[]{:S(2)}) copy-start(bf16[928,1984]{1,0:T(8,128)(2,1)} %w_qkv.1) | copy-start | bytes 11046916
  0.6 11.0 %copy-start.6 = (f32[928]{0:T(1024)S(1)}, f32[928]{0:T(1024)}, u32[]{:S(2)}) copy-start(f32[928]{0:T(1024)} %param.17) | copy-start | bytes 11140
  0.7 11.0 %copy-start.5 = (f32[928]{0:T(1024)S(1)}, f32[928]{0:T(1024)}, u32[]{:S(2)}) copy-start(f32[928]{0:T(1024)} %param.16) | copy-start | bytes 11140
  0.7 11.0 %copy-start.8 = (f32[928]{0:T(1024)S(1)}, f32[928]{0:T(1024)}, u32[]{:S(2)}) copy-start(f32[928]{0:T(1024)} %param.15) | copy-start | bytes 11140
  0.7 11.0 %copy-start.7 = (f32[928]{0:T(1024)S(1)}, f32[928]{0:T(1024)}, u32[]{:S(2)}) copy-start(f32[928]{0:T(1024)} %param.14) | copy-start | bytes 11140
  0.7 2.6 %collective-permute-start = (bf16[64,116]{1,0:T(8,128)(2,1)}, bf16[64,116]{1,0:T(8,128)(2,1)S(1)}, u32[]{:S(2)}, u32[]{:S(2)}) collective-permute-start(bf16[64,116]{1,0:T(8,128)(2,1)} %tokens.1), channel_id=1, source_target_pairs={{0,16},{16,0},{32,48},{48,32},{64,80},{80,64},{96,112},{112,96},{1... | collective-permute-start | bytes 44552 | tf_op jit(solution)/shard_map/ppermute | solution.py:51
  2.2 9.5 %copy-start = (bf16[928,3712]{1,0:T(8,128)(2,1)S(1)}, bf16[928,3712]{1,0:T(8,128)(2,1)}, u32[]{:S(2)}) copy-start(bf16[928,3712]{1,0:T(8,128)(2,1)} %w_up.1) | copy-start | bytes 20668420
  3.2 5.0 %collective-permute-start.3 = (bf16[2,64,116]{2,1,0:T(8,128)(2,1)S(1)}, bf16[2,64,116]{2,1,0:T(8,128)(2,1)S(1)}, u32[]{:S(2)}, u32[]{:S(2)}) collective-permute-start(bf16[2,64,116]{2,1,0:T(8,128)(2,1)S(1)} %pair.1.g0), channel_id=1, source_target_pairs={{0,96},{16,112},{32,0},{48,16},{64,32},{80,48},{96,64},{112,80},{1... | collective-permute-start | bytes 89096 | tf_op jit(solution)/shard_map/ppermute | solution.py:55
  7.3 4.3 %collective-permute-start.2 = (bf16[2,64,116]{2,1,0:T(8,128)(2,1)S(1)}, bf16[2,64,116]{2,1,0:T(8,128)(2,1)S(1)}, u32[]{:S(2)}, u32[]{:S(2)}) collective-permute-start(bf16[2,64,116]{2,1,0:T(8,128)(2,1)S(1)} %pair.1.g0), channel_id=1, source_target_pairs={{0,64},{16,80},{32,96},{48,112},{64,0},{80,16},{96,32},{112,48},{1... | collective-permute-start | bytes 89096 | tf_op jit(solution)/shard_map/ppermute | solution.py:55
  7.3 4.3 %collective-permute-start.1 = (bf16[2,64,116]{2,1,0:T(8,128)(2,1)S(1)}, bf16[2,64,116]{2,1,0:T(8,128)(2,1)S(1)}, u32[]{:S(2)}, u32[]{:S(2)}) collective-permute-start(bf16[2,64,116]{2,1,0:T(8,128)(2,1)S(1)} %pair.1.g0), channel_id=1, source_target_pairs={{0,32},{16,48},{32,64},{48,80},{64,96},{80,112},{96,0},{112,16},{1... | collective-permute-start | bytes 89096 | tf_op jit(solution)/shard_map/ppermute | solution.py:55
  11.6 40.8 %slice-start = ((s8[6889472]{0:T(1024)(128)(4,1)}), s8[4194304]{0:T(1024)(128)(4,1)S(1)}, s32[]{:S(2)}) async-start(s8[6889472]{0:T(1024)(128)(4,1)} %bitcast.7), calls=%async_computation.3 | async-start | bytes 8388608
  11.6 23.4 %copy-start.1 = (bf16[4,1,4096,128]{3,2,1,0:T(8,128)(2,1)S(1)}, bf16[4,1,4096,128]{3,2,1,0:T(8,128)(2,1)}, u32[]{:S(2)}) copy-start(bf16[4,1,4096,128]{3,2,1,0:T(8,128)(2,1)} %cache.1) | copy-start | bytes 12582916
  11.7 23.4 %copy-start.9 = (s32[4]{0:T(128)S(1)}, s32[4]{0:T(128)}, u32[]{:S(2)}) copy-start(s32[4]{0:T(128)} %lengths.1) | copy-start | bytes 52
  11.7 23.4 %copy-start.10 = (f32[1,128]{1,0:T(1,128)S(1)}, f32[1,128]{1,0:T(1,128)}, u32[]{:S(2)}) copy-start(f32[1,128]{1,0:T(1,128)} %constant.2.clone.inverse) | copy-start | bytes 1540
  11.7 40.7 %slice-start.1 = ((s8[6889472]{0:T(1024)(128)(4,1)}), s8[2695168]{0:T(1024)(128)(4,1)S(1)}, s32[]{:S(2)}) async-start(s8[6889472]{0:T(1024)(128)(4,1)} %bitcast.7), calls=%async_computation.4 | async-start | bytes 5390336
  35.1 17.3 %copy-start.3 = (bf16[1856,928]{0,1:T(8,128)(2,1)S(1)}, bf16[1856,928]{0,1:T(8,128)(2,1)}, u32[]{:S(2)}) copy-start(bf16[1856,928]{0,1:T(8,128)(2,1)} %param.19) | copy-start | bytes 10334212
  52.4 15.3 %copy-start.4 = (bf16[64,116]{1,0:T(8,128)(2,1)S(1)}, bf16[64,116]{1,0:T(8,128)(2,1)}, u32[]{:S(2)}) copy-start(bf16[64,116]{1,0:T(8,128)(2,1)} %tokens.1) | copy-start | bytes 44548

commit v5 on v4

--- a/solution.py
+++ b/solution.py
@@ -28,7 +28,6 @@
 PAYLOAD = AT_BIAS + QKV_BLOCKS
 RESULT = ROWS + OWN * QKV_BLOCKS
 VM = pl.BlockSpec(memory_space=pltpu.VMEM)
-SM = pl.BlockSpec(memory_space=pltpu.SMEM)
 PARAMS = pltpu.CompilerParams(vmem_limit_bytes=16 << 20)
 
 
@@ -165,7 +164,7 @@
             part = got[d, lo : lo + QKV_BLOCKS, :].astype(F32)
             acc = acc + (part + mine[:, d : d + 1] * got[d, AT_GAIN:AT_BIAS, :].astype(F32))
         qkv = (mine[:, GY : GY + 1] * acc + plain).astype(BF).astype(F32)
-        angle = lengths[r].astype(F32) * inverse[...]
+        angle = lengths[:, r : r + 1].astype(F32) * inverse[...]
         cosine = jnp.cos(angle)
         sine = jnp.sin(angle)
         sine = jnp.where(half, -sine, sine)
@@ -190,7 +189,7 @@
         scores = lax.dot_general(
             queries[r].astype(BF), cache[r, 0], (((1,), (1,)), ((), ())), preferred_element_type=F32
         )
-        return jnp.where(position < lengths[r], scores, -jnp.inf)
+        return jnp.where(position < lengths[:, r : r + 1], scores, -jnp.inf)
 
     def soften(r, scores):
         own = jnp.sum(queries[r] * keys_new[r], axis=1, keepdims=True)
@@ -262,7 +261,8 @@
         out[i] = jnp.where(first, upper, lower).astype(BF)
 
 
-def finish_kernel(shares, tokens, mixed):
+def finish_kernel(shares, tokens, held_kv, mixed, new_kv):
+    new_kv[...] = held_kv[...]
     total = shares[0].astype(F32)
     for i in range(1, 8):
         total = total + shares[i].astype(F32)
@@ -320,14 +320,14 @@
         functools.partial(middle_kernel, wide),
         out_shape=(
             jax.ShapeDtypeStruct((RESULT, BLOCK), BF),
-            jax.ShapeDtypeStruct((OWN, 2 * HD), BF),
+            pltpu.VMEM((OWN, 2 * HD), BF),
         ),
-        in_specs=[SM] + [VM] * 3,
+        in_specs=[VM] * 4,
         out_specs=(VM, VM),
         scratch_shapes=[pltpu.VMEM((LANES, LANES), F32)],
         compiler_params=PARAMS,
         name="middle",
-    )(lengths, summed, inverse, in_vmem(cache))
+    )(lengths.reshape(1, OWN), summed, inverse, in_vmem(cache))
 
     every = lax.all_to_all(jnp.broadcast_to(block[None], (GY, RESULT, BLOCK)), "gy", 0, 0)
     shares = pl.pallas_call(
@@ -344,14 +344,17 @@
         name="last",
     )(every, in_vmem(w_down.T), in_vmem(w_out.T))
 
-    mixed = pl.pallas_call(
+    mixed, new_kv = pl.pallas_call(
         finish_kernel,
-        out_shape=jax.ShapeDtypeStruct((rows, narrow), BF),
-        in_specs=[VM] * 2,
-        out_specs=VM,
+        out_shape=(
+            jax.ShapeDtypeStruct((rows, narrow), BF),
+            jax.ShapeDtypeStruct((OWN, 2 * HD), BF),
+        ),
+        in_specs=[VM] * 3,
+        out_specs=(VM, VM),
         compiler_params=pltpu.CompilerParams(vmem_limit_bytes=1 << 20),
         name="finish",
-    )(lax.all_to_all(shares, "gx", 0, 0), tokens)
+    )(lax.all_to_all(shares, "gx", 0, 0), in_vmem(mine), in_vmem(new_kv))
     return (mixed, new_kv.reshape(OWN, 1, 2 * HD))
 
 

time: 68.7 us -> 68.4 us (level)
  no operation moved by 1% of the time
where the time goes in v5:
time: 68.4 us; the launch traced here: 68.1 us
  blocking collectives  47.2 us (69%)
  Pallas kernels  9.95 us (15%)
  starting transfers between devices  6.22 us (9%)
  waiting for transfers between devices  3.8 us (6%)
  between operations  0.8 us (1%)
    all_to_all x1, blocking collectives, local(): summed = lax.all_to_all(payload, 'gy', 0, 0)  21.1 us
    all_to_all x1, blocking collectives, local(): lax.all_to_all(jnp.broadcast_to(block[None], (GY, RESULT, BLOCK)), 'gy',...  13.7 us
    all_to_all x1, blocking collectives, local(): lax.all_to_all(shares, 'gx', 0, 0)  12.3 us
    ppermute x3, starting transfers between devices, shift_z(): return lax.ppermute(x, 'gx', [(i, (i + 2 * k) % 8) for i in range(8)])  4.72 us
    ppermute x3, waiting for transfers between devices, shift_z(): return lax.ppermute(x, 'gx', [(i, (i + 2 * k) % 8) for i in range(8)])  3.63 us
    pallas_call x1, Pallas kernels, local(): pl.pallas_call(functools.partial(middle_kernel, wide), out_shape=(jax.Sha...  3.04 us
    pallas_call x1, Pallas kernels, local(): pl.pallas_call(last_kernel, out_shape=jax.ShapeDtypeStruct((8, ROWS, LANE...  3.01 us
    pallas_call x1, Pallas kernels, local(): pl.pallas_call(product_kernel, out_shape=jax.ShapeDtypeStruct((GY, PAYLOA...  2.23 us
  transfers between devices with their start and end apart: 4, of which 3 were waited for; matrix products, arithmetic and copies ran while one was open for 0% of the time, Pallas kernels for 1%

profile of v5, /device:TPU:1, one launch (start us, length us, event | category | flops | bytes accessed | tf_op | source)
XLA Modules:
  0.0 68.1 jit_solution(5366457975593845766)
XLA Ops:
  0.6 0.0 copy-start.2
  0.6 0.0 copy-start.5
  0.7 0.0 copy-start.4
  0.7 0.0 copy-start.7
  0.7 0.0 copy-start.6
  0.7 1.5 %collective-permute-start = (bf16[64,116]{1,0:T(8,128)(2,1)}, bf16[64,116]{1,0:T(8,128)(2,1)S(1)}, u32[]{:S(2)}, u32[]{:S(2)}) collective-permute-start(bf16[64,116]{1,0:T(8,128)(2,1)} %mine.1), channel_id=1, source_target_pairs={{0,16},{16,0},{32,48},{48,32},{64,80},{80,64},{96,112},{112,96},{1... | collective-permute-start | bytes 44552 | tf_op jit(solution)/shard_map/ppermute | solution.py:50
  2.2 0.0 copy-start
  2.2 0.9 %hold.1.mine.tokens = bf16[64,116]{1,0:T(8,128)(2,1)S(1)} custom-call(bf16[64,116]{1,0:T(8,128)(2,1)} %mine.1), custom_call_target="tpu_custom_call" | custom-call | flops 21474836480 | bytes 100663296 | tf_op jit(solution)/shard_map/hold/pallas_call | solution.py:280
  3.1 0.2 collective-permute-done.other
  3.2 4.0 %collective-permute-start.3 = (bf16[2,64,116]{2,1,0:T(8,128)(2,1)S(1)}, bf16[2,64,116]{2,1,0:T(8,128)(2,1)S(1)}, u32[]{:S(2)}, u32[]{:S(2)}) collective-permute-start(bf16[2,64,116]{2,1,0:T(8,128)(2,1)S(1)} %pair.1.g0), channel_id=1, source_target_pairs={{0,96},{16,112},{32,0},{48,16},{64,32},{80,48},{96,64},{112,80},{1... | collective-permute-start | bytes 89096 | tf_op jit(solution)/shard_map/ppermute | solution.py:54
  7.3 0.0 collective-permute-start.2
  7.3 0.7 %collective-permute-start.1 = (bf16[2,64,116]{2,1,0:T(8,128)(2,1)S(1)}, bf16[2,64,116]{2,1,0:T(8,128)(2,1)S(1)}, u32[]{:S(2)}, u32[]{:S(2)}) collective-permute-start(bf16[2,64,116]{2,1,0:T(8,128)(2,1)S(1)} %pair.1.g0), channel_id=1, source_target_pairs={{0,32},{16,48},{32,64},{48,80},{64,96},{80,112},{96,0},{112,16},{1... | collective-permute-start | bytes 89096 | tf_op jit(solution)/shard_map/ppermute | solution.py:54
  8.0 0.3 collective-permute-done.3.g3
  8.3 3.3 %collective-permute-done.2.g2 = bf16[2,64,116]{2,1,0:T(8,128)(2,1)S(1)} collective-permute-done((bf16[2,64,116]{2,1,0:T(8,128)(2,1)S(1)}, bf16[2,64,116]{2,1,0:T(8,128)(2,1)S(1)}, u32[]{:S(2)}, u32[]{:S(2)}) %collective-permute-start.2) | collective-permute-done | bytes 29728 | tf_op jit(solution)/shard_map/ppermute | solution.py:54
  11.6 0.0 collective-permute-done.1.g1
  11.6 0.0 slice-start
  11.6 0.0 copy-done.2
  11.6 0.0 copy-done.5
  11.6 0.0 copy-done.4
  11.6 0.0 copy-done.7
  11.6 0.0 copy-done.6
  11.6 0.0 copy-done
  11.6 0.0 copy-start.1
  11.7 0.0 copy-start.8
  11.7 0.0 copy-start.9
  11.7 0.0 slice-start.1
  11.7 2.2 %product.1 = bf16[16,120,256]{2,1,0:T(8,128)(2,1)S(1)} custom-call(bf16[2,64,116]{2,1,0:T(8,128)(2,1)S(1)} %pair.1.g0, bf16[2,64,116]{2,1,0:T(8,128)(2,1)S(1)} %collective-permute-done.1.g1, bf16[2,64,116]{2,1,0:T(8,128)(2,1)S(1)} %collective-permute-done.2.g2, bf16[2,64,116]{2,1,0:T(8,128)(2,1)S(1)} %collective-permute-done.3.g3, f32[1,928]{1,0:T(1,128)S(1)} %bitcast.12, ...), custom_call_target="tpu_custom_call" | custom-call | tf_op jit(solution)/shard_map/product/pallas_call | solution.py:301
  13.9 21.1 %all_to_all.15.got = bf16[16,120,256]{2,1,0:T(8,128)(2,1)S(1)} all-to-all(bf16[16,120,256]{2,1,0:T(8,128)(2,1)S(1)} %product.1), channel_id=1, replica_groups=mesh['gx'=8,'gy'=16] {'gy'}, dimensions={0} | all-to-all | bytes 1966080 | tf_op jit(solution)/shard_map/all_to_all | solution.py:318
  35.1 0.0 copy-start.3
  35.1 0.0 copy-done.1
  35.1 0.0 copy-done.8
  35.1 0.0 copy-done.9
  35.1 3.0 %middle.1 = (bf16[96,256]{1,0:T(8,128)(2,1)S(1)}, bf16[4,128]{1,0:T(4,128)(2,1)S(1)}) custom-call(s32[1,4]{1,0:T(1,128)S(1)} %bitcast.16, bf16[16,120,256]{2,1,0:T(8,128)(2,1)S(1)} %all_to_all.15.got, f32[1,128]{1,0:T(1,128)S(1)} %copy-done.9, bf16[4,1,4096,128]{3,2,1,0:T(8,128)(2,1)S(1)} %copy-done.1), custom_call_target="tpu_custom_call" | custom-call | tf_op jit(solution)/shard_map/middle/pallas_call | solution.py:319
  38.1 0.1 broadcast_in_dim.2
  38.2 13.7 %all_to_all.16.every = bf16[16,96,256]{2,1,0:T(8,128)(2,1)S(1)} all-to-all(bf16[16,96,256]{2,1,0:T(8,128)(2,1)S(1)} %broadcast_in_dim.2), channel_id=1, replica_groups=mesh['gx'=8,'gy'=16] {'gy'}, dimensions={0} | all-to-all | bytes 1572864 | tf_op jit(solution)/shard_map/all_to_all | solution.py:332
  52.0 0.0 slice-done
  52.0 0.0 slice-done.1
  52.0 0.0 copy-done.3
  52.0 3.0 %last.1 = bf16[8,64,128]{2,1,0:T(8,128)(2,1)S(1)} custom-call(bf16[16,96,256]{2,1,0:T(8,128)(2,1)S(1)} %all_to_all.16.every, bf16[928,3712]{1,0:T(8,128)(2,1)S(1)} %bitcast.10, bf16[928,1856]{1,0:T(8,128)(2,1)S(1)} %bitcast.11), custom_call_target="tpu_custom_call" | custom-call | tf_op jit(solution)/shard_map/last/pallas_call | solution.py:333
  55.0 12.3 %all_to_all.17.shares = bf16[8,64,128]{2,1,0:T(8,128)(2,1)S(1)} all-to-all(bf16[8,64,128]{2,1,0:T(8,128)(2,1)S(1)} %last.1), channel_id=1, replica_groups=mesh['gx'=8,'gy'=16] {'gx'}, dimensions={0} | all-to-all | bytes 262144 | tf_op jit(solution)/shard_map/all_to_all | solution.py:357
  67.3 0.8 %finish.1 = (bf16[64,116]{1,0:T(8,128)(2,1)}, bf16[4,128]{1,0:T(4,128)(2,1)}) custom-call(bf16[8,64,128]{2,1,0:T(8,128)(2,1)S(1)} %all_to_all.17.shares, bf16[64,116]{1,0:T(8,128)(2,1)S(1)} %hold.1.mine.tokens, bf16[4,128]{1,0:T(4,128)(2,1)S(1)} %get-tuple-element.7.held_kv), custom_call_target="tpu_custom_call" | custom-call | tf_op jit(solution)/shard_map/finish/pallas_call | solution.py:347
  (2 shorter events, 0.0 us)
Async XLA Ops:
  0.6 11.0 %copy-start.2 = (bf16[928,1984]{1,0:T(8,128)(2,1)S(1)}, bf16[928,1984]{1,0:T(8,128)(2,1)}, u32[]{:S(2)}) copy-start(bf16[928,1984]{1,0:T(8,128)(2,1)} %w_qkv.1) | copy-start | bytes 11046916
  0.6 11.0 %copy-start.5 = (f32[928]{0:T(1024)S(1)}, f32[928]{0:T(1024)}, u32[]{:S(2)}) copy-start(f32[928]{0:T(1024)} %param.17) | copy-start | bytes 11140
  0.7 11.0 %copy-start.4 = (f32[928]{0:T(1024)S(1)}, f32[928]{0:T(1024)}, u32[]{:S(2)}) copy-start(f32[928]{0:T(1024)} %param.16) | copy-start | bytes 11140
  0.7 11.0 %copy-start.7 = (f32[928]{0:T(1024)S(1)}, f32[928]{0:T(1024)}, u32[]{:S(2)}) copy-start(f32[928]{0:T(1024)} %param.15) | copy-start | bytes 11140
  0.7 11.0 %copy-start.6 = (f32[928]{0:T(1024)S(1)}, f32[928]{0:T(1024)}, u32[]{:S(2)}) copy-start(f32[928]{0:T(1024)} %param.14) | copy-start | bytes 11140
  0.7 2.6 %collective-permute-start = (bf16[64,116]{1,0:T(8,128)(2,1)}, bf16[64,116]{1,0:T(8,128)(2,1)S(1)}, u32[]{:S(2)}, u32[]{:S(2)}) collective-permute-start(bf16[64,116]{1,0:T(8,128)(2,1)} %mine.1), channel_id=1, source_target_pairs={{0,16},{16,0},{32,48},{48,32},{64,80},{80,64},{96,112},{112,96},{1... | collective-permute-start | bytes 44552 | tf_op jit(solution)/shard_map/ppermute | solution.py:50
  2.2 9.5 %copy-start = (bf16[928,3712]{1,0:T(8,128)(2,1)S(1)}, bf16[928,3712]{1,0:T(8,128)(2,1)}, u32[]{:S(2)}) copy-start(bf16[928,3712]{1,0:T(8,128)(2,1)} %w_up.1) | copy-start | bytes 20668420
  3.2 5.0 %collective-permute-start.3 = (bf16[2,64,116]{2,1,0:T(8,128)(2,1)S(1)}, bf16[2,64,116]{2,1,0:T(8,128)(2,1)S(1)}, u32[]{:S(2)}, u32[]{:S(2)}) collective-permute-start(bf16[2,64,116]{2,1,0:T(8,128)(2,1)S(1)} %pair.1.g0), channel_id=1, source_target_pairs={{0,96},{16,112},{32,0},{48,16},{64,32},{80,48},{96,64},{112,80},{1... | collective-permute-start | bytes 89096 | tf_op jit(solution)/shard_map/ppermute | solution.py:54
  7.3 4.3 %collective-permute-start.2 = (bf16[2,64,116]{2,1,0:T(8,128)(2,1)S(1)}, bf16[2,64,116]{2,1,0:T(8,128)(2,1)S(1)}, u32[]{:S(2)}, u32[]{:S(2)}) collective-permute-start(bf16[2,64,116]{2,1,0:T(8,128)(2,1)S(1)} %pair.1.g0), channel_id=1, source_target_pairs={{0,64},{16,80},{32,96},{48,112},{64,0},{80,16},{96,32},{112,48},{1... | collective-permute-start | bytes 89096 | tf_op jit(solution)/shard_map/ppermute | solution.py:54
  7.3 4.3 %collective-permute-start.1 = (bf16[2,64,116]{2,1,0:T(8,128)(2,1)S(1)}, bf16[2,64,116]{2,1,0:T(8,128)(2,1)S(1)}, u32[]{:S(2)}, u32[]{:S(2)}) collective-permute-start(bf16[2,64,116]{2,1,0:T(8,128)(2,1)S(1)} %pair.1.g0), channel_id=1, source_target_pairs={{0,32},{16,48},{32,64},{48,80},{64,96},{80,112},{96,0},{112,16},{1... | collective-permute-start | bytes 89096 | tf_op jit(solution)/shard_map/ppermute | solution.py:54
  11.6 40.4 %slice-start = ((s8[6889472]{0:T(1024)(128)(4,1)}), s8[4194304]{0:T(1024)(128)(4,1)S(1)}, s32[]{:S(2)}) async-start(s8[6889472]{0:T(1024)(128)(4,1)} %bitcast.8), calls=%async_computation.3 | async-start | bytes 8388608
  11.6 23.4 %copy-start.1 = (bf16[4,1,4096,128]{3,2,1,0:T(8,128)(2,1)S(1)}, bf16[4,1,4096,128]{3,2,1,0:T(8,128)(2,1)}, u32[]{:S(2)}) copy-start(bf16[4,1,4096,128]{3,2,1,0:T(8,128)(2,1)} %cache.1) | copy-start | bytes 12582916
  11.7 23.4 %copy-start.8 = (s32[4]{0:T(128)S(1)}, s32[4]{0:T(128)}, u32[]{:S(2)}) copy-start(s32[4]{0:T(128)} %param.13) | copy-start | bytes 52
  11.7 23.4 %copy-start.9 = (f32[1,128]{1,0:T(1,128)S(1)}, f32[1,128]{1,0:T(1,128)}, u32[]{:S(2)}) copy-start(f32[1,128]{1,0:T(1,128)} %constant.2.clone.inverse) | copy-start | bytes 1540
  11.7 40.3 %slice-start.1 = ((s8[6889472]{0:T(1024)(128)(4,1)}), s8[2695168]{0:T(1024)(128)(4,1)S(1)}, s32[]{:S(2)}) async-start(s8[6889472]{0:T(1024)(128)(4,1)} %bitcast.8), calls=%async_computation.4 | async-start | bytes 5390336
  35.1 16.9 %copy-start.3 = (bf16[1856,928]{0,1:T(8,128)(2,1)S(1)}, bf16[1856,928]{0,1:T(8,128)(2,1)}, u32[]{:S(2)}) copy-start(bf16[1856,928]{0,1:T(8,128)(2,1)} %param.19) | copy-start | bytes 10334212

commit v6 on v5

--- a/solution.py
+++ b/solution.py
@@ -238,19 +238,19 @@
         for h in range(2):
             cols = slice(h * LANES, (h + 1) * LANES)
             spread[h, d * step : (d + 1) * step, :] = every[d, ROWS:, cols].astype(F32)
+    both = (((1,), (1,)), ((), ()))
+    total = None
     for d, (at, size) in enumerate(chunks(up_cols, BLOCK)):
         part = every[d, :ROWS, :size]
-        left[:ROWS, at : at + size] = part
-        left[ROWS:, at : at + size] = part
-    for t in range(-(-attn_cols // LANES)):
+        part = jnp.concatenate([part, part], axis=0)
+        one = lax.dot_general(w_down[:, at : at + size], part, both, preferred_element_type=F32)
+        total = one if total is None else total + one
+    for t, (at, size) in enumerate(chunks(attn_cols, LANES)):
         part = spread[t % 2, pl.ds(t // 2, ROWS, stride=QKV_BLOCKS), :].astype(BF)
-        at = up_cols + t * LANES
         left[:ROWS, at : at + LANES] = part
         left[ROWS:, at : at + LANES] = part
-    both = (((1,), (1,)), ((), ()))
-    total = lax.dot_general(w_down[...], left[:, :up_cols], both, preferred_element_type=F32)
     total = total + lax.dot_general(
-        w_out[...], left[:, up_cols : up_cols + attn_cols], both, preferred_element_type=F32
+        w_out[...], left[:, :attn_cols], both, preferred_element_type=F32
     )
     turned[: 8 * narrow, :] = total
     turned[8 * narrow :, :] = jnp.zeros((turned.shape[0] - 8 * narrow, LANES), F32)
@@ -337,7 +337,7 @@
         out_specs=VM,
         scratch_shapes=[
             pltpu.VMEM((2, rows * QKV_BLOCKS, LANES), F32),
-            pltpu.VMEM((2 * rows, w_down.shape[0] + 15 * LANES), BF),
+            pltpu.VMEM((2 * rows, 15 * LANES), BF),
             pltpu.VMEM((8 * narrow + 16, LANES), F32),
         ],
         compiler_params=PARAMS,

time: 68.4 us -> 68.3 us (level)
  no operation moved by 1% of the time
where the time goes in v6:
time: 68.3 us; the launch traced here: 68 us
  blocking collectives  47.2 us (69%)
  Pallas kernels  9.86 us (14%)
  starting transfers between devices  6.22 us (9%)
  waiting for transfers between devices  3.8 us (6%)
  between operations  0.8 us (1%)
    all_to_all x1, blocking collectives, local(): summed = lax.all_to_all(payload, 'gy', 0, 0)  21.1 us
    all_to_all x1, blocking collectives, local(): lax.all_to_all(jnp.broadcast_to(block[None], (GY, RESULT, BLOCK)), 'gy',...  13.7 us
    all_to_all x1, blocking collectives, local(): lax.all_to_all(shares, 'gx', 0, 0)  12.3 us
    ppermute x3, starting transfers between devices, shift_z(): return lax.ppermute(x, 'gx', [(i, (i + 2 * k) % 8) for i in range(8)])  4.72 us
    ppermute x3, waiting for transfers between devices, shift_z(): return lax.ppermute(x, 'gx', [(i, (i + 2 * k) % 8) for i in range(8)])  3.63 us
    pallas_call x1, Pallas kernels, local(): pl.pallas_call(functools.partial(middle_kernel, wide), out_shape=(jax.Sha...  3.04 us
    pallas_call x1, Pallas kernels, local(): pl.pallas_call(last_kernel, out_shape=jax.ShapeDtypeStruct((8, ROWS, LANE...  2.92 us
    pallas_call x1, Pallas kernels, local(): pl.pallas_call(product_kernel, out_shape=jax.ShapeDtypeStruct((GY, PAYLOA...  2.23 us
  transfers between devices with their start and end apart: 4, of which 3 were waited for; matrix products, arithmetic and copies ran while one was open for 0% of the time, Pallas kernels for 1%

profile of v6, /device:TPU:1, one launch (start us, length us, event | category | flops | bytes accessed | tf_op | source)
XLA Modules:
  0.0 68.0 jit_solution(12476668516771221932)
XLA Ops:
  0.6 0.0 copy-start.2
  0.6 0.0 copy-start.5
  0.7 0.0 copy-start.4
  0.7 0.0 copy-start.7
  0.7 0.0 copy-start.6
  0.7 1.5 %collective-permute-start = (bf16[64,116]{1,0:T(8,128)(2,1)}, bf16[64,116]{1,0:T(8,128)(2,1)S(1)}, u32[]{:S(2)}, u32[]{:S(2)}) collective-permute-start(bf16[64,116]{1,0:T(8,128)(2,1)} %mine.1), channel_id=1, source_target_pairs={{0,16},{16,0},{32,48},{48,32},{64,80},{80,64},{96,112},{112,96},{1... | collective-permute-start | bytes 44552 | tf_op jit(solution)/shard_map/ppermute | solution.py:50
  2.2 0.0 copy-start
  2.2 0.9 %hold.1.mine.tokens = bf16[64,116]{1,0:T(8,128)(2,1)S(1)} custom-call(bf16[64,116]{1,0:T(8,128)(2,1)} %mine.1), custom_call_target="tpu_custom_call" | custom-call | flops 21474836480 | bytes 100663296 | tf_op jit(solution)/shard_map/hold/pallas_call | solution.py:280
  3.1 0.2 collective-permute-done.other
  3.2 4.0 %collective-permute-start.3 = (bf16[2,64,116]{2,1,0:T(8,128)(2,1)S(1)}, bf16[2,64,116]{2,1,0:T(8,128)(2,1)S(1)}, u32[]{:S(2)}, u32[]{:S(2)}) collective-permute-start(bf16[2,64,116]{2,1,0:T(8,128)(2,1)S(1)} %pair.1.g0), channel_id=1, source_target_pairs={{0,96},{16,112},{32,0},{48,16},{64,32},{80,48},{96,64},{112,80},{1... | collective-permute-start | bytes 89096 | tf_op jit(solution)/shard_map/ppermute | solution.py:54
  7.3 0.0 collective-permute-start.2
  7.3 0.7 %collective-permute-start.1 = (bf16[2,64,116]{2,1,0:T(8,128)(2,1)S(1)}, bf16[2,64,116]{2,1,0:T(8,128)(2,1)S(1)}, u32[]{:S(2)}, u32[]{:S(2)}) collective-permute-start(bf16[2,64,116]{2,1,0:T(8,128)(2,1)S(1)} %pair.1.g0), channel_id=1, source_target_pairs={{0,32},{16,48},{32,64},{48,80},{64,96},{80,112},{96,0},{112,16},{1... | collective-permute-start | bytes 89096 | tf_op jit(solution)/shard_map/ppermute | solution.py:54
  8.0 0.3 collective-permute-done.3.g3
  8.3 3.3 %collective-permute-done.2.g2 = bf16[2,64,116]{2,1,0:T(8,128)(2,1)S(1)} collective-permute-done((bf16[2,64,116]{2,1,0:T(8,128)(2,1)S(1)}, bf16[2,64,116]{2,1,0:T(8,128)(2,1)S(1)}, u32[]{:S(2)}, u32[]{:S(2)}) %collective-permute-start.2) | collective-permute-done | bytes 29728 | tf_op jit(solution)/shard_map/ppermute | solution.py:54
  11.6 0.0 collective-permute-done.1.g1
  11.6 0.0 slice-start
  11.6 0.0 copy-done.2
  11.6 0.0 copy-done.5
  11.6 0.0 copy-done.4
  11.6 0.0 copy-done.7
  11.6 0.0 copy-done.6
  11.6 0.0 copy-done
  11.6 0.0 copy-start.1
  11.7 0.0 copy-start.8
  11.7 0.0 copy-start.9
  11.7 0.0 slice-start.1
  11.7 2.2 %product.1 = bf16[16,120,256]{2,1,0:T(8,128)(2,1)S(1)} custom-call(bf16[2,64,116]{2,1,0:T(8,128)(2,1)S(1)} %pair.1.g0, bf16[2,64,116]{2,1,0:T(8,128)(2,1)S(1)} %collective-permute-done.1.g1, bf16[2,64,116]{2,1,0:T(8,128)(2,1)S(1)} %collective-permute-done.2.g2, bf16[2,64,116]{2,1,0:T(8,128)(2,1)S(1)} %collective-permute-done.3.g3, f32[1,928]{1,0:T(1,128)S(1)} %bitcast.12, ...), custom_call_target="tpu_custom_call" | custom-call | tf_op jit(solution)/shard_map/product/pallas_call | solution.py:301
  13.9 21.1 %all_to_all.15.got = bf16[16,120,256]{2,1,0:T(8,128)(2,1)S(1)} all-to-all(bf16[16,120,256]{2,1,0:T(8,128)(2,1)S(1)} %product.1), channel_id=1, replica_groups=mesh['gx'=8,'gy'=16] {'gy'}, dimensions={0} | all-to-all | bytes 1966080 | tf_op jit(solution)/shard_map/all_to_all | solution.py:318
  35.1 0.0 copy-start.3
  35.1 0.0 copy-done.1
  35.1 0.0 copy-done.8
  35.1 0.0 copy-done.9
  35.1 3.0 %middle.1 = (bf16[96,256]{1,0:T(8,128)(2,1)S(1)}, bf16[4,128]{1,0:T(4,128)(2,1)S(1)}) custom-call(s32[1,4]{1,0:T(1,128)S(1)} %bitcast.16, bf16[16,120,256]{2,1,0:T(8,128)(2,1)S(1)} %all_to_all.15.got, f32[1,128]{1,0:T(1,128)S(1)} %copy-done.9, bf16[4,1,4096,128]{3,2,1,0:T(8,128)(2,1)S(1)} %copy-done.1), custom_call_target="tpu_custom_call" | custom-call | tf_op jit(solution)/shard_map/middle/pallas_call | solution.py:319
  38.1 0.1 broadcast_in_dim.2
  38.2 13.7 %all_to_all.16.every = bf16[16,96,256]{2,1,0:T(8,128)(2,1)S(1)} all-to-all(bf16[16,96,256]{2,1,0:T(8,128)(2,1)S(1)} %broadcast_in_dim.2), channel_id=1, replica_groups=mesh['gx'=8,'gy'=16] {'gy'}, dimensions={0} | all-to-all | bytes 1572864 | tf_op jit(solution)/shard_map/all_to_all | solution.py:332
  52.0 0.0 slice-done
  52.0 0.0 slice-done.1
  52.0 0.0 copy-done.3
  52.0 2.9 %last.1 = bf16[8,64,128]{2,1,0:T(8,128)(2,1)S(1)} custom-call(bf16[16,96,256]{2,1,0:T(8,128)(2,1)S(1)} %all_to_all.16.every, bf16[928,3712]{1,0:T(8,128)(2,1)S(1)} %bitcast.10, bf16[928,1856]{1,0:T(8,128)(2,1)S(1)} %bitcast.11), custom_call_target="tpu_custom_call" | custom-call | tf_op jit(solution)/shard_map/last/pallas_call | solution.py:333
  54.9 12.3 %all_to_all.17.shares = bf16[8,64,128]{2,1,0:T(8,128)(2,1)S(1)} all-to-all(bf16[8,64,128]{2,1,0:T(8,128)(2,1)S(1)} %last.1), channel_id=1, replica_groups=mesh['gx'=8,'gy'=16] {'gx'}, dimensions={0} | all-to-all | bytes 262144 | tf_op jit(solution)/shard_map/all_to_all | solution.py:357
  67.2 0.8 %finish.1 = (bf16[64,116]{1,0:T(8,128)(2,1)}, bf16[4,128]{1,0:T(4,128)(2,1)}) custom-call(bf16[8,64,128]{2,1,0:T(8,128)(2,1)S(1)} %all_to_all.17.shares, bf16[64,116]{1,0:T(8,128)(2,1)S(1)} %hold.1.mine.tokens, bf16[4,128]{1,0:T(4,128)(2,1)S(1)} %get-tuple-element.7.held_kv), custom_call_target="tpu_custom_call" | custom-call | tf_op jit(solution)/shard_map/finish/pallas_call | solution.py:347
  (2 shorter events, 0.0 us)
Async XLA Ops:
  0.6 11.0 %copy-start.2 = (bf16[928,1984]{1,0:T(8,128)(2,1)S(1)}, bf16[928,1984]{1,0:T(8,128)(2,1)}, u32[]{:S(2)}) copy-start(bf16[928,1984]{1,0:T(8,128)(2,1)} %w_qkv.1) | copy-start | bytes 11046916
  0.6 11.0 %copy-start.5 = (f32[928]{0:T(1024)S(1)}, f32[928]{0:T(1024)}, u32[]{:S(2)}) copy-start(f32[928]{0:T(1024)} %param.17) | copy-start | bytes 11140
  0.7 11.0 %copy-start.4 = (f32[928]{0:T(1024)S(1)}, f32[928]{0:T(1024)}, u32[]{:S(2)}) copy-start(f32[928]{0:T(1024)} %param.16) | copy-start | bytes 11140
  0.7 11.0 %copy-start.7 = (f32[928]{0:T(1024)S(1)}, f32[928]{0:T(1024)}, u32[]{:S(2)}) copy-start(f32[928]{0:T(1024)} %param.15) | copy-start | bytes 11140
  0.7 11.0 %copy-start.6 = (f32[928]{0:T(1024)S(1)}, f32[928]{0:T(1024)}, u32[]{:S(2)}) copy-start(f32[928]{0:T(1024)} %param.14) | copy-start | bytes 11140
  0.7 2.6 %collective-permute-start = (bf16[64,116]{1,0:T(8,128)(2,1)}, bf16[64,116]{1,0:T(8,128)(2,1)S(1)}, u32[]{:S(2)}, u32[]{:S(2)}) collective-permute-start(bf16[64,116]{1,0:T(8,128)(2,1)} %mine.1), channel_id=1, source_target_pairs={{0,16},{16,0},{32,48},{48,32},{64,80},{80,64},{96,112},{112,96},{1... | collective-permute-start | bytes 44552 | tf_op jit(solution)/shard_map/ppermute | solution.py:50
  2.2 9.5 %copy-start = (bf16[928,3712]{1,0:T(8,128)(2,1)S(1)}, bf16[928,3712]{1,0:T(8,128)(2,1)}, u32[]{:S(2)}) copy-start(bf16[928,3712]{1,0:T(8,128)(2,1)} %w_up.1) | copy-start | bytes 20668420
  3.2 5.0 %collective-permute-start.3 = (bf16[2,64,116]{2,1,0:T(8,128)(2,1)S(1)}, bf16[2,64,116]{2,1,0:T(8,128)(2,1)S(1)}, u32[]{:S(2)}, u32[]{:S(2)}) collective-permute-start(bf16[2,64,116]{2,1,0:T(8,128)(2,1)S(1)} %pair.1.g0), channel_id=1, source_target_pairs={{0,96},{16,112},{32,0},{48,16},{64,32},{80,48},{96,64},{112,80},{1... | collective-permute-start | bytes 89096 | tf_op jit(solution)/shard_map/ppermute | solution.py:54
  7.3 4.3 %collective-permute-start.2 = (bf16[2,64,116]{2,1,0:T(8,128)(2,1)S(1)}, bf16[2,64,116]{2,1,0:T(8,128)(2,1)S(1)}, u32[]{:S(2)}, u32[]{:S(2)}) collective-permute-start(bf16[2,64,116]{2,1,0:T(8,128)(2,1)S(1)} %pair.1.g0), channel_id=1, source_target_pairs={{0,64},{16,80},{32,96},{48,112},{64,0},{80,16},{96,32},{112,48},{1... | collective-permute-start | bytes 89096 | tf_op jit(solution)/shard_map/ppermute | solution.py:54
  7.3 4.3 %collective-permute-start.1 = (bf16[2,64,116]{2,1,0:T(8,128)(2,1)S(1)}, bf16[2,64,116]{2,1,0:T(8,128)(2,1)S(1)}, u32[]{:S(2)}, u32[]{:S(2)}) collective-permute-start(bf16[2,64,116]{2,1,0:T(8,128)(2,1)S(1)} %pair.1.g0), channel_id=1, source_target_pairs={{0,32},{16,48},{32,64},{48,80},{64,96},{80,112},{96,0},{112,16},{1... | collective-permute-start | bytes 89096 | tf_op jit(solution)/shard_map/ppermute | solution.py:54
  11.6 40.4 %slice-start = ((s8[6889472]{0:T(1024)(128)(4,1)}), s8[4194304]{0:T(1024)(128)(4,1)S(1)}, s32[]{:S(2)}) async-start(s8[6889472]{0:T(1024)(128)(4,1)} %bitcast.8), calls=%async_computation.3 | async-start | bytes 8388608
  11.6 23.4 %copy-start.1 = (bf16[4,1,4096,128]{3,2,1,0:T(8,128)(2,1)S(1)}, bf16[4,1,4096,128]{3,2,1,0:T(8,128)(2,1)}, u32[]{:S(2)}) copy-start(bf16[4,1,4096,128]{3,2,1,0:T(8,128)(2,1)} %cache.1) | copy-start | bytes 12582916
  11.7 23.4 %copy-start.8 = (s32[4]{0:T(128)S(1)}, s32[4]{0:T(128)}, u32[]{:S(2)}) copy-start(s32[4]{0:T(128)} %param.13) | copy-start | bytes 52
  11.7 23.4 %copy-start.9 = (f32[1,128]{1,0:T(1,128)S(1)}, f32[1,128]{1,0:T(1,128)}, u32[]{:S(2)}) copy-start(f32[1,128]{1,0:T(1,128)} %constant.2.clone.inverse) | copy-start | bytes 1540
  11.7 40.3 %slice-start.1 = ((s8[6889472]{0:T(1024)(128)(4,1)}), s8[2695168]{0:T(1024)(128)(4,1)S(1)}, s32[]{:S(2)}) async-start(s8[6889472]{0:T(1024)(128)(4,1)} %bitcast.8), calls=%async_computation.4 | async-start | bytes 5390336
  35.1 16.9 %copy-start.3 = (bf16[1856,928]{0,1:T(8,128)(2,1)S(1)}, bf16[1856,928]{0,1:T(8,128)(2,1)}, u32[]{:S(2)}) copy-start(bf16[1856,928]{0,1:T(8,128)(2,1)} %param.19) | copy-start | bytes 10334212
